TPU v7x, 32 devices: a whole 2x2x4 slice. The times are simulated.
32 devices in a mesh: fsdp: 4 (over x, core), ctx: 8 (over z, y).
Axes of the slice: x: 2, y: 2, z: 4, core: 2. Of those that a mesh axis runs over, the one named last changes fastest.
Arguments:
- hidden: bfloat16 [4, 1024, 2304], P('fsdp', 'ctx'), may hold values from -6 to 6
- query_heads: bfloat16 [4, 1024, 2048], P('fsdp', 'ctx'), may hold values from -6 to 6
- key_heads: bfloat16 [4, 1024, 2048], P('fsdp', 'ctx'), may hold values from -6 to 6
- value_heads: bfloat16 [4, 1024, 2048], P('fsdp', 'ctx'), may hold values from -6 to 6
- out_grad: bfloat16 [4, 1024, 2048], P('fsdp', 'ctx'), may hold values from -6 to 6
- checkpoint: float32 [4, 8, 16, 128, 128], P('fsdp', 'ctx'), may hold values from -6 to 6
- gate_down: bfloat16 [2304, 128], P('fsdp'), may hold values from -0.125 to 0.125
- gate_up: bfloat16 [128, 2048], P(None, 'fsdp'), may hold values from -0.5 to 0.5
- gate_bias: float32 [2048], replicated, may hold values from -4 to 4
- decay_rate: float32 [2048], replicated, may hold values from 0.0001953125 to 0.05
- beta_weight: bfloat16 [2304, 16], P('fsdp'), may hold values from -0.125 to 0.125
Outputs:
- query_grad: bfloat16 [4, 1024, 2048], P('fsdp', 'ctx')
- key_grad: bfloat16 [4, 1024, 2048], P('fsdp', 'ctx')
- value_grad: bfloat16 [4, 1024, 2048], P('fsdp', 'ctx')
- hidden_grad: bfloat16 [4, 1024, 2304], P('fsdp', 'ctx')
- gate_down_grad: float32 [2304, 128], P('fsdp')
- gate_up_grad: float32 [128, 2048], P(None, 'fsdp')
- beta_weight_grad: float32 [2304, 16], P('fsdp')
- gate_bias_grad: float32 [2048], replicated
- decay_rate_grad: float32 [2048], replicated
All inputs are finite; a program needn't handle non-finite values.
Results may differ from a plain program's by a relative error of at most 0.0052.
Values may be sent and summed in bfloat16 or wider, within the bound.
A program may use at most 256 MiB of HBM per device.

v0:
```python
import jax
import jax.numpy as jnp
from jax import lax
from jax.sharding import PartitionSpec as P

CH = 128


PRECISE = lax.Precision.HIGHEST
EPSILON = 1e-06


def carried_in(value, axis, join, neutral):
    count, mine = (lax.axis_size(axis), lax.axis_index(axis))
    pieces = jax.tree.map(lambda part: lax.all_gather(part, axis), value)
    pieces = jax.tree.map(lambda part: part[::-1], pieces)
    mine = count - 1 - mine
    so_far = jax.tree.map(
        lambda part, zero: jnp.full_like(part, 0) + jnp.asarray(zero, part.dtype), value, neutral
    )

    def turn(position, so_far):
        longer = join(so_far, jax.tree.map(lambda part: part[position], pieces))
        return jax.tree.map(lambda new, old: jnp.where(position < mine, new, old), longer, so_far)

    return lax.fori_loop(0, count - 1, turn, so_far)


def unit_rows(matrix):
    return matrix * lax.rsqrt(jnp.sum(matrix * matrix, axis=-1, keepdims=True) + EPSILON)


def to_spans(values):
    tok_rows = values.shape[0]
    return values.reshape((tok_rows // CH, CH) + values.shape[1:]).swapaxes(1, 2)


def tri_masks():
    row_index = lax.broadcasted_iota(jnp.int32, (CH, CH), 0)
    col_index = lax.broadcasted_iota(jnp.int32, (CH, CH), 1)
    return (
        (row_index > col_index).astype(jnp.float32),
        (row_index >= col_index).astype(jnp.float32),
    )


def span_terms(k_span, g_span, b_span):
    cumulative = jnp.cumsum(g_span, axis=1)
    key_plus = k_span * jnp.exp(cumulative)
    key_minus = k_span * jnp.exp(-cumulative)
    key_end = k_span * jnp.exp(cumulative[:, -1:, :] - cumulative)
    strict, _ = tri_masks()
    mixing = (
        jnp.einsum("htc,hsc->hts", key_plus, key_minus, precision=PRECISE)
        * strict
        * b_span[:, :, None]
    )
    system = mixing + jnp.eye(CH, dtype=jnp.float32)
    return (cumulative, key_plus, key_minus, key_end, system)


def block_forward(start_state, queries, keys_in, values_in, decay_heads, beta_gate):
    q_all = to_spans(unit_rows(queries))
    k_all = to_spans(unit_rows(keys_in))
    v_all = to_spans(values_in)
    g_all = to_spans(decay_heads)
    b_all = to_spans(beta_gate)
    _, inclusive = tri_masks()

    def block_advance(carried, pieces):
        q_span, k_span, v_span, g_span, b_span = pieces
        cumulative, key_plus, key_minus, key_end, system = span_terms(k_span, g_span, b_span)
        query_plus = q_span * jnp.exp(cumulative)
        target = b_span[:, :, None] * (
            v_span - jnp.einsum("htc,hcd->htd", key_plus, carried, precision=PRECISE)
        )
        updates = jax.scipy.linalg.solve_triangular(system, target, lower=True, unit_diagonal=True)
        scores = jnp.einsum("htc,hsc->hts", query_plus, key_minus, precision=PRECISE) * inclusive
        outputs = jnp.einsum("htc,hcd->htd", query_plus, carried, precision=PRECISE) + jnp.einsum(
            "hts,hsd->htd", scores, updates, precision=PRECISE
        )
        renewed = jnp.exp(cumulative[:, -1, :])[:, :, None] * carried + jnp.einsum(
            "hsc,hsd->hcd", key_end, updates, precision=PRECISE
        )
        return (renewed, outputs)

    end_state, outputs = lax.scan(block_advance, start_state, (q_all, k_all, v_all, g_all, b_all))
    return (outputs.swapaxes(1, 2).reshape(queries.shape), end_state)


def transition(keys_in, decay_heads, beta_gate, identity):
    k_all = to_spans(unit_rows(keys_in))
    g_all = to_spans(decay_heads)
    b_all = to_spans(beta_gate)

    def transition_advance(product, pieces):
        k_span, g_span, b_span = pieces
        cumulative, key_plus, key_minus, key_end, system = span_terms(k_span, g_span, b_span)
        solved = jax.scipy.linalg.solve_triangular(
            system, b_span[:, :, None] * key_plus, lower=True, unit_diagonal=True
        )
        moving = jnp.exp(cumulative[:, -1, :])[:, :, None] * identity - jnp.einsum(
            "hsc,hse->hce", key_end, solved, precision=PRECISE
        )
        return (jnp.einsum("hce,hef->hcf", moving, product, precision=PRECISE), None)

    result, _ = lax.scan(transition_advance, identity, (k_all, g_all, b_all))
    return result


def combine(earlier, later):
    first_map, first_sum = earlier
    second_map, second_sum = later
    joined_map = jnp.einsum("hab,hbc->hac", first_map, second_map, precision=PRECISE)
    joined_sum = jnp.einsum("hba,hbc->hac", second_map, first_sum, precision=PRECISE) + second_sum
    return (joined_map, joined_sum)


def gate_forward(hidden_rows, down_full, up_full, gate_bias, decay_rate, beta_full):
    low_rank = jnp.dot(hidden_rows, down_full, preferred_element_type=jnp.float32).astype(
        jnp.bfloat16
    )
    gate_input = jnp.dot(low_rank, up_full, preferred_element_type=jnp.float32) + gate_bias
    log_decay = -decay_rate * jax.nn.softplus(gate_input)
    beta_gate = jax.nn.sigmoid(jnp.dot(hidden_rows, beta_full, preferred_element_type=jnp.float32))
    return (low_rank, gate_input, log_decay, beta_gate)


def contract_rows(left, right):
    return lax.dot_general(
        left, right, (((0,), (0,)), ((), ())), preferred_element_type=jnp.float32
    )


def contract_cols(left, right):
    return lax.dot_general(
        left, right, (((1,), (1,)), ((), ())), preferred_element_type=jnp.float32
    )


def gate_backward(
    hidden_rows,
    low_rank,
    gate_input,
    beta_gate,
    decay_cot,
    beta_cot,
    down_full,
    up_full,
    decay_rate,
    beta_full,
):
    input_grad = decay_cot * -decay_rate * jax.nn.sigmoid(gate_input)
    input_half = input_grad.astype(jnp.bfloat16)
    rate_term = -jnp.sum(decay_cot * jax.nn.softplus(gate_input), axis=0)
    bias_term = jnp.sum(input_grad, axis=0)
    up_term = contract_rows(low_rank, input_half)
    low_grad = contract_cols(input_half, up_full).astype(jnp.bfloat16)
    score_grad = (beta_cot * beta_gate * (1.0 - beta_gate)).astype(jnp.bfloat16)
    down_term = contract_rows(hidden_rows, low_grad)
    beta_term = contract_rows(hidden_rows, score_grad)
    hidden_grad = (
        contract_cols(low_grad, down_full) + contract_cols(score_grad, beta_full)
    ).astype(jnp.bfloat16)
    return (hidden_grad, down_term, up_term, beta_term, bias_term, rate_term)


def on_device(
    hidden,
    query_heads,
    key_heads,
    value_heads,
    out_grad,
    checkpoint,
    gate_down,
    gate_up,
    gate_bias,
    decay_rate,
    beta_weight,
):
    tok_rows, model_width = (hidden.shape[1], hidden.shape[2])
    count_heads, size_head = (checkpoint.shape[2], checkpoint.shape[3])
    down_full, beta_full, up_full = (
        lax.all_gather(gate_down, "fsdp", axis=0, tiled=True),
        lax.all_gather(beta_weight, "fsdp", axis=0, tiled=True),
        lax.all_gather(gate_up, "fsdp", axis=1, tiled=True),
    )
    hidden_rows = hidden.reshape(tok_rows, model_width)
    low_rank, gate_input, log_decay, beta_gate = gate_forward(
        hidden_rows, down_full, up_full, gate_bias, decay_rate, beta_full
    )

    def per_head(values):
        return values.reshape(tok_rows, count_heads, size_head).astype(jnp.float32)

    start_state = checkpoint.reshape(count_heads, size_head, size_head)
    keys_in = per_head(key_heads)
    decay_heads = log_decay.reshape(tok_rows, count_heads, size_head)
    _, pullback = jax.vjp(
        block_forward,
        start_state,
        per_head(query_heads),
        keys_in,
        per_head(value_heads),
        decay_heads,
        beta_gate,
    )
    cotangent = per_head(out_grad)
    local_sum = pullback((cotangent, jnp.zeros_like(start_state)))[0]
    identity = jnp.broadcast_to(jnp.eye(size_head, dtype=jnp.float32), start_state.shape)
    moving = transition(keys_in, decay_heads, beta_gate, identity)
    _, end_grad = carried_in(
        (moving, local_sum), "ctx", combine, (identity, jnp.zeros_like(start_state))
    )
    start_grad, q_grad, k_grad, v_grad, decay_cot, beta_cot = pullback((cotangent, end_grad))
    hidden_grad, down_term, up_term, beta_term, bias_term, rate_term = gate_backward(
        hidden_rows,
        low_rank,
        gate_input,
        beta_gate,
        decay_cot.reshape(tok_rows, -1),
        beta_cot,
        down_full,
        up_full,
        decay_rate,
        beta_full,
    )
    local_parts = (
        lax.psum_scatter(down_term, "fsdp", scatter_dimension=0, tiled=True),
        lax.psum_scatter(beta_term, "fsdp", scatter_dimension=0, tiled=True),
        lax.psum_scatter(up_term, "fsdp", scatter_dimension=1, tiled=True),
    )
    shards = lax.psum((local_parts[0], local_parts[1], local_parts[2]), "ctx")
    vectors = lax.psum((bias_term, rate_term), ("fsdp", "ctx"))

    def restore(values):
        return values.reshape(1, tok_rows, -1).astype(jnp.bfloat16)

    return (
        restore(q_grad),
        restore(k_grad),
        restore(v_grad),
        hidden_grad.reshape(1, tok_rows, model_width),
        shards[0],
        shards[2],
        shards[1],
        vectors[0],
        vectors[1],
    )


def solution(mesh):
    return jax.shard_map(
        on_device,
        mesh=mesh,
        in_specs=(
            P("fsdp", "ctx", None),
            P("fsdp", "ctx", None),
            P("fsdp", "ctx", None),
            P("fsdp", "ctx", None),
            P("fsdp", "ctx", None),
            P("fsdp", "ctx", None, None, None),
            P("fsdp", None),
            P(None, "fsdp"),
            P(),
            P(),
            P("fsdp", None),
        ),
        out_specs=(
            P("fsdp", "ctx", None),
            P("fsdp", "ctx", None),
            P("fsdp", "ctx", None),
            P("fsdp", "ctx", None),
            P("fsdp", None),
            P(None, "fsdp"),
            P("fsdp", None),
            P(),
            P(),
        ),
        check_vma=False,
    )
```

profile of v0, /device:TPU:0, one launch (start us, length us, event | category | flops | bytes accessed | tf_op | source)
XLA Modules:
  0.0 749.4 jit_solution(8032928988702432763)
XLA Ops:
  12.5 9.1 %all_gather.21 = bf16[2304,128]{1,0:T(8,128)(2,1)S(1)} all-gather(bf16[576,128]{1,0:T(8,128)(2,1)S(1)} %copy-done.42), channel_id=1, replica_groups=mesh['fsdp'=4,'ctx'=8] {'fsdp'}, dimensions={0}, use_global_device_ids=true | all-gather | bytes 737280 | tf_op jit(solution)/shard_map/all_gather | solution.py:184
  21.6 7.3 all_gather.22
  31.1 23.2 %fusion.20 = f32[16,128,128]{2,0,1:T(8,128)S(1)} fusion(f32[1,128,16,128]{3,2,1,0:T(8,128)S(1)} %bitcast.382), kind=kOutput, calls=%fused_computation.48 | output fusion | flops 33292288 | bytes 2097152 | tf_op jit(solution)/shard_map/jvp()/while/body/eval_jaxpr/jit(cumsum)/reduce_window_sum | solution.py:48
  59.8 2.9 convolution_multiply_fusion.1
  66.7 4.1 convolution_multiply_fusion.2
  70.8 5.5 all-gather.2
  82.1 158.6 %custom-call.10 = f32[16,1,128,128]{2,3,1,0:T(8,128)} custom-call(f32[16,1,128,128]{3,2,1,0:T(8,128)} %add_bitcast_fusion), custom_call_target="InvertDiagBlocksLowerTriangular" | custom-call | tf_op jit(solution)/shard_map/jvp()/while/body/eval_jaxpr/jit(_solve_triangular)/vmap()/triangular_solve/custom-call.1 | solution.py:77
  240.7 3.2 convolution_add_fusion.8
  245.2 3.4 convolution_add_fusion.6
  248.6 3.8 fusion.47
  278.1 3.3 convolution_add_fusion.9
  281.5 93.1 %all-gather.8.cloned.1.call-done = f32[128,128,128]{2,1,0:T(8,128)} async-done(((f32[16,128,128]{2,1,0:T(8,128)}), f32[128,128,128]{2,1,0:T(8,128)}) %all-gather.8.cloned.1.call-update) | async-done | bytes 8388624 | tf_op jit(solution)/shard_map/all_gather | solution.py:15
  374.5 7.8 %rev.7 = f32[8,16,128,128]{3,2,1,0:T(8,128)} reverse(f32[8,16,128,128]{3,2,1,0:T(8,128)} %bitcast.378), dimensions={0} | reverse | bytes 16777216 | tf_op jit(solution)/shard_map/rev | solution.py:16
  382.3 117.5 %all-gather.6.cloned.1.call-done = f32[128,128,128]{2,1,0:T(8,128)} async-done(((f32[16,128,128]{2,1,0:T(8,128)}), f32[128,128,128]{2,1,0:T(8,128)}) %all-gather.6.cloned.1.call-update) | async-done | bytes 8388624 | tf_op jit(solution)/shard_map/all_gather | solution.py:15
  499.8 9.1 %copy.143 = f32[8,16,128,128]{2,3,1,0:T(8,128)} copy(f32[8,16,128,128]{3,2,1,0:T(8,128)} %bitcast.379) | data formatting | bytes 16777216 | tf_op jit(solution)/shard_map/all_gather | solution.py:15
  508.9 7.8 %rev.6 = f32[8,16,128,128]{2,3,1,0:T(8,128)} reverse(f32[8,16,128,128]{2,3,1,0:T(8,128)} %copy.143), dimensions={0} | reverse | bytes 16777216 | tf_op jit(solution)/shard_map/rev | solution.py:16
  516.7 35.5 %while.10 = (s32[]{:T(128)}, f32[16,128,128]{2,1,0:T(8,128)}, s32[]{:T(128)}, f32[8,16,128,128]{2,3,1,0:T(8,128)}, f32[8,16,128,128]{3,2,1,0:T(8,128)}, /*index=5*/s32[]{:T(128)}, s32[]{:T(128)}) while((s32[]{:T(128)}, f32[16,128,128]{2,1,0:T(8,128)}, s32[]{:T(128)}, f32[8,16,128,128]{2,3,1,0:T(8,128)}, ...), condition=%wide.region_5.8_spmd.clone, body=%wide.region_4.7_spmd.clone.sunk | while | flops 403701760 | bytes 7342687 | solution.py:26
  517.9 3.8 fusion.166
  523.0 3.8 fusion.166
  528.0 3.8 fusion.166
  533.0 3.8 fusion.166
  538.1 3.8 fusion.166
  543.1 3.8 fusion.166
  548.2 3.8 fusion.166
  552.2 3.2 convolution_add_fusion.5
  567.6 2.8 convolution_add_fusion.4
  570.4 3.8 fusion.21
  586.6 19.8 %reduce-scatter.10.cloned.1.call-done = f32[576,128]{1,0:T(8,128)} async-done(((f32[2304,128]{1,0:T(8,128)}), f32[576,128]{1,0:T(8,128)}) %reduce-scatter.10.cloned.1.call-update) | async-done | bytes 294928
  608.2 25.6 %reduce-scatter.8.cloned.1.call-done = f32[128,512]{1,0:T(8,128)} async-done(((f32[128,2048]{1,0:T(8,128)}), f32[128,512]{1,0:T(8,128)}) %reduce-scatter.8.cloned.1.call-update) | async-done | bytes 262160 | tf_op jit(solution)/shard_map/reduce_scatter | solution.py:231
  640.4 39.4 %all-reduce.2 = (f32[2048]{0:T(1024)}, f32[2048]{0:T(1024)}) all-reduce(f32[2048]{0:T(1024)S(1)} %get-tuple-element.431, f32[2048]{0:T(1024)S(1)} %neg.70), channel_id=1, replica_groups=mesh['fsdp'=4,'ctx'=8] {'fsdp','ctx'}, use_global_device_ids=true, to_apply=%region_19.22 | all-reduce | flops 4096 | bytes 32768 | tf_op jit(solution)/shard_map/psum | solution.py:234
  682.4 38.6 %psum.37 = f32[576,16]{0,1:T(8,128)} all-reduce(f32[576,16]{0,1:T(8,128)S(1)} %copy.206), channel_id=1, replica_groups=mesh['fsdp'=4,'ctx'=8] {'ctx'}, use_global_device_ids=true, to_apply=%region_17.20 | all-reduce | flops 9216 | bytes 73728 | tf_op jit(solution)/shard_map/psum | solution.py:233
  721.0 17.9 %all-reduce.6.cloned.1.call-done = (f32[576,128]{0,1:T(8,128)}, f32[128,512]{1,0:T(8,128)}) async-done(((f32[576,128]{0,1:T(8,128)}, f32[128,512]{1,0:T(8,128)}), (f32[576,128]{0,1:T(8,128)}, f32[128,512]{1,0:T(8,128)})) %all-reduce.6.cloned.1.call-update) | async-done | bytes 557072 | tf_op jit(solution)/shard_map/psum | solution.py:233
  (200 shorter events, 96.7 us)
Async XLA Ops:
  7.2 21.8 %copy-start = (bf16[1,128,2304]{2,1,0:T(8,128)(2,1)S(1)}, bf16[1,128,2304]{2,1,0:T(8,128)(2,1)}, u32[]{:S(2)}) copy-start(bf16[1,128,2304]{2,1,0:T(8,128)(2,1)} %param.17) | copy-start | bytes 1769476
  7.2 367.3 %all-gather.8.cloned.1.call-start = ((), (), s32[]{:S(2)}) async-start(), calls=%async_computation.5 | async-start | bytes 9437184 | tf_op jit(solution)/shard_map/all_gather | solution.py:15
  11.2 48.4 %copy-start.44 = (f32[128,16]{0,1:T(8,128)}, f32[128,16]{0,1:T(8,128)S(1)}, u32[]{:S(2)}) copy-start(f32[128,16]{0,1:T(8,128)S(1)} %multiply_reduce_fusion.2) | copy-start | bytes 24580
  11.6 17.4 %copy-start.13 = (f32[1,128,2048]{1,2,0:T(8,128)}, f32[1,128,2048]{1,2,0:T(8,128)S(1)}, u32[]{:S(2)}) copy-start(f32[1,128,2048]{1,2,0:T(8,128)S(1)} %convert_element_type.168) | copy-start | bytes 3145732
  11.6 10.1 %copy-start.43 = (bf16[128,512]{1,0:T(8,128)(2,1)S(1)}, bf16[128,512]{1,0:T(8,128)(2,1)}, u32[]{:S(2)}) copy-start(bf16[128,512]{1,0:T(8,128)(2,1)} %param.24) | copy-start | bytes 393220
  11.6 17.4 %copy-start.51 = (f32[2048]{0:T(1024)S(1)}, f32[2048]{0:T(1024)}, u32[]{:S(2)}) copy-start(f32[2048]{0:T(1024)} %param.26) | copy-start | bytes 24580
  12.5 47.0 %copy-start.46 = (f32[128,16]{0,1:T(8,128)}, f32[128,16]{0,1:T(8,128)S(1)}, u32[]{:S(2)}) copy-start(f32[128,16]{0,1:T(8,128)S(1)} %multiply_reduce_fusion.3) | copy-start | bytes 24580
  12.5 17.2 %copy-start.50 = (f32[2048]{0:T(1024)S(1)}, f32[2048]{0:T(1024)}, u32[]{:S(2)}) copy-start(f32[2048]{0:T(1024)} %param.25) | copy-start | bytes 24580
  21.6 7.3 copy-start.24
  59.8 2.9 copy-start.23
  66.6 4.1 copy-start.49
  240.7 3.2 copy-start.2
  240.7 3.2 copy-start.36
  248.6 251.2 %all-gather.6.cloned.1.call-start = ((), (), s32[]{:S(2)}) async-start(), calls=%async_computation.4 | async-start | bytes 9437184 | tf_op jit(solution)/shard_map/all_gather | solution.py:15
  248.6 3.8 copy-start.48
  257.0 349.3 %reduce-scatter.10.cloned.1.call-start = ((), (), s32[]{:S(2)}) async-start(), calls=%async_computation.6 | async-start | bytes 1474560
  267.0 2.6 copy-start.8
  267.0 2.6 copy-start.35
  552.1 3.3 copy-start.1
  552.2 3.3 copy-start.11
  555.4 2.6 copy-start.4
  559.2 2.7 copy-start.16
  564.3 3.3 copy-start.37
  567.6 2.8 copy-start.21
  567.6 2.8 copy-start.32
  567.6 2.8 copy-start.34
  570.4 3.8 copy-start.7
  582.3 51.5 %reduce-scatter.8.cloned.1.call-start = ((), (), s32[]{:S(2)}) async-start(), calls=%async_computation.3 | async-start | bytes 1310720 | tf_op jit(solution)/shard_map/reduce_scatter | solution.py:231
  583.7 97.6 %reduce-scatter.12.cloned.1.call-start = ((), (), s32[]{:S(2)}) async-start(), calls=%async_computation.7 | async-start | bytes 1474560
  586.5 47.4 %copy-start.45 = (f32[128,16]{0,1:T(8,128)S(1)}, f32[128,16]{0,1:T(8,128)}, u32[]{:S(2)}) copy-start(f32[128,16]{0,1:T(8,128)} %copy-done.44) | copy-start | bytes 24580
  586.5 152.3 %all-reduce.6.cloned.1.call-start = ((), (), s32[]{:S(2)}) async-start(), calls=%async_computation.8 | async-start | bytes 1179648 | tf_op jit(solution)/shard_map/psum | solution.py:233
  639.1 40.7 %copy-start.25 = (bf16[2304,128]{1,0:T(8,128)(2,1)S(1)}, bf16[2304,128]{1,0:T(8,128)(2,1)}, u32[]{:S(2)}) copy-start(bf16[2304,128]{1,0:T(8,128)(2,1)} %copy-done.24) | copy-start | bytes 1769476
  (26 other events, 36.7 us)
Sparse Core Ops, SparseCore 0:
  248.7 125.7 all-gather.7
  376.7 123.1 all-gather.5
  582.4 23.9 reduce-scatter.9
  608.9 24.8 reduce-scatter.7
  636.3 25.7 reduce-scatter.11
  665.7 73.0 all-reduce.5
where the time goes:
time: 758 us; the launch traced here: 749 us
  waiting for transfers between devices  274 us (36%)
  other arithmetic  196 us (26%)
  blocking collectives  99.9 us (13%)
  matrix products  91.4 us (12%)
  local copies, waits for them, and re-layouts  72.1 us (10%)
  between operations  15.2 us (2%)
    all_gather x2, waiting for transfers between devices, carried_in(): pieces = jax.tree.map(lambda part: lax.all_gather(part, axis), value)  211 us
    another operation x5, other arithmetic, block_advance(): jax.scipy.linalg.solve_triangular(system, target, lower=True, unit_diagon...  163 us
    psum x1, blocking collectives, on_device(): vectors = lax.psum((bias_term, rate_term), ('fsdp', 'ctx'))  39.4 us
    psum x1, blocking collectives, on_device(): shards = lax.psum((local_parts[0], local_parts[1], local_parts[2]), 'ctx')  38.6 us
    another operation x3, other arithmetic, span_terms(): cumulative = jnp.cumsum(g_span, axis=1)  28.1 us
    dot_general x7, matrix products, combine(): jnp.einsum('hba,hbc->hac', second_map, first_sum, precision=PRECISE)  26.7 us
    reduce_scatter x1, waiting for transfers between devices, on_device(): lax.psum_scatter(up_term, 'fsdp', scatter_dimension=1, tiled=True)  25.6 us
    unnamed x118, local copies, waits for them, and re-layouts  24.1 us
  transfers between devices with their start and end apart: 6, of which 5 were waited for; matrix products, arithmetic and copies ran while one was open for 7% of the time, Pallas kernels for 0%

commit v1 on v0

v1 whole, which is shorter than its diff:
```python
import functools

import jax
import jax.numpy as jnp
from jax import lax
from jax.experimental import pallas as pl
from jax.experimental.pallas import tpu as pltpu
from jax.sharding import PartitionSpec as P

EPSILON = 1e-06
MESH = pl.DeviceIdType.MESH
F32, BF16 = jnp.float32, jnp.bfloat16
VMEM_LIMIT = 48 * 1024 * 1024
NN, NT, TN = ((1,), (0,)), ((1,), (1,)), ((0,), (0,))
INV_PASSES = 1
PASSES = 3


def dot(left, right, dims=NN):
    return lax.dot_general(left, right, (dims, ((), ())), preferred_element_type=F32)


def halves(value):
    if value.dtype == BF16:
        return value, None
    high = value.astype(BF16)
    return high, (value - high.astype(F32)).astype(BF16)


def mm(left, right, dims=NN, passes=None):
    passes = PASSES if passes is None else passes
    if passes == 1:
        return dot(left.astype(BF16), right.astype(BF16), dims)
    left_high, left_low = halves(left)
    right_high, right_low = halves(right)
    total = dot(left_high, right_high, dims)
    if left_low is not None:
        total += dot(left_low, right_high, dims)
    if right_low is not None:
        total += dot(left_high, right_low, dims)
    return total


def sum_by(ones, value):
    high = value.astype(BF16)
    rest = value - high.astype(F32)
    mid = rest.astype(BF16)
    low = (rest - mid.astype(F32)).astype(BF16)
    return dot(ones, high) + dot(ones, mid) + dot(ones, low)


def iotas(size):
    return (
        lax.broadcasted_iota(jnp.int32, (size, size), 0),
        lax.broadcasted_iota(jnp.int32, (size, size), 1),
    )


def inverse(systems):
    size = systems[0].shape[0]
    row, col = iotas(size)
    eye = jnp.where(row == col, 1.0, 0.0)

    def off(block):
        same = row // (2 * block) == col // (2 * block)
        return same & ((row // block) % 2 == 1) & ((col // block) % 2 == 0)

    found = [eye - jnp.where(off(1), system, 0.0) for system in systems]
    block = 2
    while block < size:
        mask = off(block)
        parts = [mm(jnp.where(mask, s, 0.0), t, NN, INV_PASSES) for s, t in zip(systems, found)]
        found = [t - mm(t, p, NN, INV_PASSES) for t, p in zip(found, parts)]
        block *= 2
    return found


def softplus(value):
    return jnp.maximum(value, 0.0) + jnp.log1p(jnp.exp(-jnp.abs(value)))


def sigmoid(value):
    return 1.0 / (1.0 + jnp.exp(-value))


def unit(rows):
    scale = lax.rsqrt(jnp.sum(rows * rows, axis=-1, keepdims=True) + EPSILON)
    return rows * scale, scale


def unit_back(grad, rows, scale):
    return scale * (grad - rows * jnp.sum(grad * rows, axis=-1, keepdims=True))


def head_terms(keys, gate_in, rate):
    size = keys.shape[0]
    row, col = iotas(size)
    kn, k_scale = unit(keys.astype(F32))
    ones = jnp.where(row >= col, 1.0, 0.0).astype(BF16)
    cumulative = sum_by(ones, -rate * softplus(gate_in))
    return kn, k_scale, cumulative


def local_heads(heads):
    row, col = iotas(heads[0]["k"].shape[0])
    for h in heads:
        kn, _, cum = head_terms(h["k"], h["gate_in"], h["rate"])
        qn, q_scale = unit(h["q"].astype(F32))
        plus = jnp.exp(cum)
        h.update(cum=cum, qn=qn, q_scale=q_scale, plus=plus)
        h.update(kp=kn * plus, km=kn * jnp.exp(-cum), qp=qn * plus)
        h.update(ke=kn * jnp.exp(cum[-1:] - cum), gf=h["go"].astype(F32))
    for h in heads:
        h["kk"] = jnp.where(row > col, mm(h["kp"], h["km"], NT), 0.0)
        h["p"] = jnp.where(row >= col, mm(h["qp"], h["km"], NT), 0.0)
    for h, t in zip(heads, inverse([h["kk"] * h["beta"] for h in heads])):
        h["t"] = t
    for h in heads:
        h["r"] = h["v"].astype(F32) - mm(h["kp"], h["s"])
        h["pg"] = mm(h["p"], h["go"], TN)
    for h in heads:
        h["u"] = mm(h["t"], h["beta"] * h["r"])
        h["wa"] = mm(h["t"], h["ke"], TN)
        h["wb"] = mm(h["t"], h["pg"], TN)
    for h in heads:
        kb = h["kp"] * h["beta"]
        end = jnp.exp(h["cum"][-1:])
        h["map"] = jnp.where(row == col, end, 0.0) - mm(kb, h["wa"], TN)
        h["add"] = mm(h["qp"], h["go"], TN) - mm(kb, h["wb"], TN)
        h["dp"] = jnp.where(row >= col, mm(h["go"], h["u"], NT), 0.0)
    for h in heads:
        dqp = mm(h["go"], h["s"], NT) + mm(h["dp"], h["km"])
        h["dq"] = unit_back(dqp * h["plus"], h["qn"], h["q_scale"])
        h["dcum"] = dqp * h["qp"]
        h["dkm"] = mm(h["dp"], h["qp"], TN)
    return heads


def back_heads(heads):
    size = heads[0]["k"].shape[0]
    row, col = iotas(size)
    ones = jnp.where(row <= col, 1.0, 0.0).astype(BF16)
    for h in heads:
        kn, k_scale = unit(h["k"].astype(F32))
        cum = h["cum"]
        plus, minus, end = jnp.exp(cum), jnp.exp(-cum), jnp.exp(cum[-1:] - cum)
        h.update(kn=kn, k_scale=k_scale, plus=plus, minus=minus, end=end, kp=kn * plus)
        h["w"] = h["wb"] + mm(h["wa"], h["x"])
    for h in heads:
        h["dv"] = h["beta"] * h["w"]
        h["dm"] = jnp.where(row > col, -mm(h["w"], h["u"], NT), 0.0)
        h["dke"] = mm(h["u"], h["x"], NT)
    for h in heads:
        kn = h["kn"]
        km, ke = kn * h["minus"], kn * h["end"]
        dmb = h["beta"] * h["dm"]
        h["dbeta"] = jnp.sum(h["w"] * h["r"] + h["dm"] * h["kk"], axis=1, keepdims=True)
        dkp = mm(dmb, km) - mm(h["dv"], h["s"], NT)
        dkm = mm(dmb, h["kp"], TN) + h["dkm"]
        ended = h["dke"] * ke
        kept = jnp.sum((h["x"] * h["s"]).T, axis=0, keepdims=True) * jnp.exp(h["cum"][-1:])
        last = jnp.sum(ended, axis=0, keepdims=True) + kept
        dcum = h["dcum"] + dkp * h["kp"] - dkm * km - ended
        h["dg"] = sum_by(ones, dcum) + last
        grad = dkp * h["plus"] + dkm * h["minus"] + h["dke"] * h["end"]
        h["dk"] = unit_back(grad, kn, h["k_scale"])
    for h in heads:
        gate = sigmoid(h["gate_in"])
        h["dgate"] = h["dg"] * -h["rate"] * gate
        h["rate_row"] = -jnp.sum(h["dg"] * softplus(h["gate_in"]), axis=0, keepdims=True)
        h["bias_row"] = jnp.sum(h["dgate"], axis=0, keepdims=True)
    return heads


def column(table, index):
    lanes = lax.broadcasted_iota(jnp.int32, table.shape, 1)
    return jnp.sum(jnp.where(lanes == index, table, 0.0), axis=1, keepdims=True)


def local_kernel(
    group, hidden, down, up, beta_t, bias, rate, q, k, v, go, s,
    low, gates, dq, cum, wa, wb, u, r, kk, dcum, dkm, maps, adds,
):
    size = s.shape[-1]
    step = pl.program_id(0)

    @pl.when(step == 0)
    def _():
        low[...] = dot(hidden[...], down[...]).astype(BF16)
        gates[...] = sigmoid(dot(hidden[...], beta_t[...], NT))

    heads = []
    for i in range(group):
        at = slice(i * size, (i + 1) * size)
        heads.append(
            dict(
                q=q[:, at], k=k[:, at], v=v[:, at], go=go[:, at], s=s[i],
                gate_in=dot(low[...], up[i]) + bias[:, at],
                rate=rate[:, at],
                beta=column(gates[...], step * group + i),
            )
        )
    for i, h in enumerate(local_heads(heads)):
        at = slice(i * size, (i + 1) * size)
        dq[:, at] = h["dq"].astype(BF16)
        cum[i], wa[i], wb[i], u[i], r[i] = h["cum"], h["wa"].astype(BF16), h["wb"], h["u"].astype(BF16), h["r"]
        kk[i], dcum[i], dkm[i] = h["kk"], h["dcum"], h["dkm"]
        maps[i], adds[i] = h["map"], h["add"]


def back_kernel(
    group, shards, steps,
    hidden, down, up, beta_t, bias, rate, k, s, low, gates, x, cum, wa, wb, u, r, kk, dcum, dkm,
    dk, dv, dhidden, packed,
    low_sum, beta_cot, rows,
):
    size = s.shape[-1]
    count = group * steps
    step = pl.program_id(0)
    per_shard = count // shards
    deep = down.shape[0] // shards
    first_rep = deep + per_shard * size
    lanes = lax.broadcasted_iota(jnp.int32, beta_cot.shape, 1)

    @pl.when(step == 0)
    def _():
        low_sum[...] = jnp.zeros_like(low_sum)
        beta_cot[...] = jnp.zeros_like(beta_cot)

    heads = []
    for i in range(group):
        at = slice(i * size, (i + 1) * size)
        heads.append(
            dict(
                k=k[:, at], s=s[i], x=x[i].astype(F32),
                gate_in=dot(low[...], up[i]) + bias[:, at],
                rate=rate[:, at],
                beta=column(gates[...], step * group + i),
                cum=cum[i], wa=wa[i], wb=wb[i], u=u[i], r=r[i], kk=kk[i], dcum=dcum[i], dkm=dkm[i],
            )
        )
    for i, h in enumerate(back_heads(heads)):
        at = slice(i * size, (i + 1) * size)
        head = step * group + i
        dk[:, at] = h["dk"].astype(BF16)
        dv[:, at] = h["dv"].astype(BF16)
        half = h["dgate"].astype(BF16)
        place = pl.multiple_of(deep + (head % per_shard) * size, 16)
        packed[head // per_shard, pl.ds(place, size), :] = dot(low[...], half, TN).astype(BF16)
        low_sum[...] += dot(half, up[i], NT)
        beta_cot[...] += jnp.where(lanes == head, h["dbeta"], 0.0)
        rows[pl.ds(head, 1), :] = h["bias_row"]
        rows[pl.ds(count + head, 1), :] = h["rate_row"]

    @pl.when(step == steps - 1)
    def _():
        low_grad = low_sum[...].astype(BF16)
        gate = gates[...]
        score = (beta_cot[...] * gate * (1.0 - gate)).astype(BF16)
        dhidden[...] = (dot(low_grad, down[...], NT) + dot(score, beta_t[...])).astype(BF16)
        down_term = dot(hidden[...], low_grad, TN).astype(BF16)
        beta_term = dot(score, hidden[...], TN).astype(BF16)
        tail = rows[...].astype(BF16)
        blocks = hidden.shape[1] // size
        for shard in range(shards):
            packed[shard, :deep, :] = down_term[shard * deep : (shard + 1) * deep]
            for b in range(blocks):
                place = first_rep + b * count
                packed[shard, place : place + count, :] = beta_term[:, b * size : (b + 1) * size]
            place = first_rep + blocks * count
            packed[shard, place : place + 2 * count, :] = tail
            if place + 2 * count < packed.shape[1]:
                rest = packed.shape[1] - place - 2 * count
                packed[shard, place + 2 * count :, :] = jnp.zeros((rest, packed.shape[2]), BF16)


def chain_kernel(count, maps, adds, out, sent, got, send_sem, recv_sem):
    me = lax.axis_index("ctx")
    barrier = pltpu.get_barrier_semaphore()

    @pl.when(me > 0)
    def _():
        pl.semaphore_signal(barrier, inc=1, device_id={"ctx": me - 1}, device_id_type=MESH)

    @pl.when(me < count - 1)
    def _():
        pl.semaphore_signal(barrier, inc=1, device_id={"ctx": me + 1}, device_id_type=MESH)

    @pl.when((me > 0) & (me < count - 1))
    def _():
        pl.semaphore_wait(barrier, 2)

    @pl.when((me == 0) | (me == count - 1))
    def _():
        pl.semaphore_wait(barrier, 1)

    @pl.when(me == count - 1)
    def _():
        got[...] = jnp.zeros_like(got)

    def copy(head):
        return pltpu.make_async_remote_copy(
            src_ref=sent.at[head], dst_ref=got.at[head],
            send_sem=send_sem.at[head], recv_sem=recv_sem.at[head],
            device_id={"ctx": jnp.maximum(me - 1, 0)}, device_id_type=MESH,
        )

    def turn(head, _):
        @pl.when(me < count - 1)
        def _():
            copy(head).wait_recv()

        value = got[head]
        out[head] = value

        @pl.when(me > 0)
        def _():
            sent[head] = (adds[head] + mm(maps[head], value, NN, 3)).astype(BF16)
            copy(head).start()

        return 0

    lax.fori_loop(0, maps.shape[0], turn, 0)

    @pl.when(me > 0)
    def _():
        def done(head, _):
            copy(head).wait_send()
            return 0

        lax.fori_loop(0, maps.shape[0], done, 0)


def gather_kernel(shards, down, up, beta, down_all, up_all, beta_all, send_sem, recv_sem):
    me = lax.axis_index("fsdp")
    chips = shards // 2
    chip, core = me // 2, me % 2
    sibling = chip * 2 + (1 - core)
    peers = [lax.rem(chip + d, chips) * 2 + core for d in range(1, chips)]
    sources = [lax.rem(chip + chips - d, chips) * 2 + core for d in range(1, chips)]
    barrier = pltpu.get_barrier_semaphore()
    for other in [sibling] + peers:
        pl.semaphore_signal(barrier, inc=1, device_id={"fsdp": other}, device_id_type=MESH)
    size = up_all.shape[-1]
    for i in range(up.shape[1] // size):
        up_all[me, i] = up[:, i * size : (i + 1) * size]
    down_all[me] = down[...]
    beta_all[me] = beta[...]
    pl.semaphore_wait(barrier, chips)

    def copies(shard, target, slot):
        return [
            pltpu.make_async_remote_copy(
                src_ref=ref.at[shard], dst_ref=ref.at[shard],
                send_sem=send_sem.at[slot, i], recv_sem=recv_sem.at[slot, i],
                device_id={"fsdp": target}, device_id_type=MESH,
            )
            for i, ref in enumerate((down_all, up_all, beta_all))
        ]

    for d, peer in enumerate(peers):
        for c in copies(me, peer, 1 + d):
            c.start()
    for c in copies(me, sibling, 0):
        c.start()
    for d, source in enumerate(sources):
        for c, onward in zip(copies(source, peers[d], 1 + d), copies(source, sibling, chips + d)):
            c.wait_recv()
            onward.start()
    for c in copies(sibling, sibling, 0):
        c.wait_recv()
    for d, source in enumerate(sources):
        theirs = (source // 2) * 2 + (1 - core)
        for c in copies(theirs, sibling, chips + d):
            c.wait_recv()
    for slot in range(2 * chips - 1):
        for c in copies(me, sibling, slot):
            c.wait_send()


def reduce_kernel(
    shards, count, packed, out,
    core_got, core_sum, chip_got, chip_sum, piece_got, total, spread,
    core_send, core_recv, chip_send, chip_recv, piece_send, piece_recv, spread_send, spread_recv,
):
    me, mine = lax.axis_index("fsdp"), lax.axis_index("ctx")
    chips = shards // 2
    chip, core = me // 2, me % 2
    sibling = chip * 2 + (1 - core)
    peers = [lax.rem(chip + d, chips) * 2 + core for d in range(1, chips)]
    others = [lax.rem(mine + d, count) for d in range(1, count)]
    piece = packed.shape[1] // count
    barrier = pltpu.get_barrier_semaphore()
    for other in [sibling] + peers:
        pl.semaphore_signal(barrier, inc=1, device_id={"fsdp": other}, device_id_type=MESH)

    def greet(d, _):
        pl.semaphore_signal(
            barrier, inc=1, device_id={"ctx": lax.rem(mine + d, count)}, device_id_type=MESH
        )
        return 0

    lax.fori_loop(1, count, greet, 0)
    pl.semaphore_wait(barrier, chips + count - 1)

    def core_copy(c):
        return pltpu.make_async_remote_copy(
            src_ref=packed.at[c * 2 + (1 - core)], dst_ref=core_got.at[c],
            send_sem=core_send.at[c], recv_sem=core_recv.at[c],
            device_id={"fsdp": sibling}, device_id_type=MESH,
        )

    def chip_copy(d, peer):
        return pltpu.make_async_remote_copy(
            src_ref=core_sum.at[peer // 2], dst_ref=chip_got.at[d],
            send_sem=chip_send.at[d], recv_sem=chip_recv.at[d],
            device_id={"fsdp": peer}, device_id_type=MESH,
        )

    order = [peer // 2 for peer in peers] + [chip]
    for c in order:
        core_copy(c).start()
    for d, c in enumerate(order):
        core_copy(c).wait_recv()
        both = packed[c * 2 + core].astype(F32) + core_got[c].astype(F32)
        if d < chips - 1:
            core_sum[c] = both.astype(BF16)
            chip_copy(d, peers[d]).start()
        else:
            own = both
    for d in range(chips - 1):
        chip_copy(d, peers[d]).wait_recv()
        own = own + chip_got[d].astype(F32)
    chip_sum[...] = own.astype(BF16)

    def piece_copy(d):
        other = lax.rem(mine + d, count)
        at = pl.multiple_of(other * piece, 16)
        return pltpu.make_async_remote_copy(
            src_ref=chip_sum.at[pl.ds(at, piece)], dst_ref=piece_got.at[d - 1],
            send_sem=piece_send.at[d - 1], recv_sem=piece_recv.at[d - 1],
            device_id={"ctx": other}, device_id_type=MESH,
        )

    def spread_copy(d):
        return pltpu.make_async_remote_copy(
            src_ref=total, dst_ref=spread.at[d - 1],
            send_sem=spread_send.at[d - 1], recv_sem=spread_recv.at[d - 1],
            device_id={"ctx": lax.rem(mine + d, count)}, device_id_type=MESH,
        )

    def start_piece(d, _):
        piece_copy(d).start()
        return 0

    def add_piece(d, so_far):
        piece_copy(d).wait_recv()
        return so_far + piece_got[d - 1].astype(F32)

    def start_spread(d, _):
        spread_copy(d).start()
        return 0

    def place_spread(d, _):
        spread_copy(d).wait_recv()
        source = lax.rem(mine + count - d, count)
        out[pl.ds(pl.multiple_of(source * piece, 16), piece), :] = spread[d - 1].astype(F32)
        return 0

    def finish(d, _):
        piece_copy(d).wait_send()
        spread_copy(d).wait_send()
        return 0

    lax.fori_loop(1, count, start_piece, 0)
    at = pl.multiple_of(mine * piece, 16)
    summed = lax.fori_loop(1, count, add_piece, chip_sum[pl.ds(at, piece), :].astype(F32))
    total[...] = summed.astype(BF16)
    lax.fori_loop(1, count, start_spread, 0)
    out[pl.ds(at, piece), :] = total[...].astype(F32)
    lax.fori_loop(1, count, place_spread, 0)
    lax.fori_loop(1, count, finish, 0)
    for c in range(chips):
        core_copy(c).wait_send()
    for d, peer in enumerate(peers):
        chip_copy(d, peer).wait_send()


def vmem(count):
    return [pl.BlockSpec(memory_space=pltpu.VMEM)] * count


def remote(collective):
    return pltpu.CompilerParams(
        collective_id=collective, has_side_effects=True, vmem_limit_bytes=VMEM_LIMIT
    )


def on_device(
    shards, blocks_ctx,
    hidden, query_heads, key_heads, value_heads, out_grad, checkpoint,
    gate_down, gate_up, gate_bias, decay_rate, beta_weight,
):
    tokens, width = hidden.shape[1], hidden.shape[2]
    count, size = checkpoint.shape[2], checkpoint.shape[3]
    rank = gate_down.shape[1]
    deep = gate_down.shape[0]
    per_shard = count // shards
    chips = shards // 2
    hidden, q, k, v, go = (a[0] for a in (hidden, query_heads, key_heads, value_heads, out_grad))
    state = checkpoint[0, 0]
    bias, rate = gate_bias.reshape(1, -1), decay_rate.reshape(1, -1)
    dma = pltpu.SemaphoreType.DMA

    down_all, up_all, beta_all = pl.pallas_call(
        functools.partial(gather_kernel, shards),
        out_shape=(
            jax.ShapeDtypeStruct((shards, deep, rank), BF16),
            jax.ShapeDtypeStruct((shards, per_shard, rank, size), BF16),
            jax.ShapeDtypeStruct((shards, count, deep), BF16),
        ),
        in_specs=vmem(3),
        out_specs=tuple(vmem(3)),
        scratch_shapes=[dma((2 * chips - 1, 3)), dma((2 * chips - 1, 3))],
        compiler_params=remote(0),
        name="gather_weights",
    )(gate_down, gate_up, beta_weight.T)
    down_full = down_all.reshape(width, rank)
    up_full = up_all.reshape(count, rank, size)
    beta_t = beta_all.swapaxes(0, 1).reshape(count, width)

    group = 4 if count % 4 == 0 else 1
    steps = count // group
    whole = lambda *shape: pl.BlockSpec(shape, lambda i: (0,) * len(shape))
    cols = pl.BlockSpec((tokens, group * size), lambda i: (0, i))
    line = pl.BlockSpec((1, group * size), lambda i: (0, i))
    per_head = lambda a, b: pl.BlockSpec((group, a, b), lambda i: (i, 0, 0))
    of_heads = lambda a, b, kind: jax.ShapeDtypeStruct((count, a, b), kind)
    weights = [
        whole(tokens, width), whole(width, rank), per_head(rank, size), whole(count, width), line, line
    ]
    square = per_head(tokens, size)
    grid_params = pltpu.CompilerParams(
        dimension_semantics=("arbitrary",), vmem_limit_bytes=VMEM_LIMIT
    )
    low, gates, dq, cum, wa, wb, u, r, kk, dcum, dkm, maps, adds = pl.pallas_call(
        functools.partial(local_kernel, group),
        grid=(steps,),
        out_shape=(
            jax.ShapeDtypeStruct((tokens, rank), BF16),
            jax.ShapeDtypeStruct((tokens, count), F32),
            jax.ShapeDtypeStruct((tokens, count * size), BF16),
            of_heads(tokens, size, F32), of_heads(tokens, size, BF16), of_heads(tokens, size, F32),
            of_heads(tokens, size, BF16), of_heads(tokens, size, F32), of_heads(tokens, tokens, F32),
            of_heads(tokens, size, F32), of_heads(tokens, size, F32),
            of_heads(size, size, F32), of_heads(size, size, F32),
        ),
        in_specs=weights + [cols] * 4 + [per_head(size, size)],
        out_specs=(
            whole(tokens, rank), whole(tokens, count), cols,
            square, square, square, square, square, per_head(tokens, tokens), square, square,
            per_head(size, size), per_head(size, size),
        ),
        compiler_params=grid_params,
        name="local_terms",
    )(hidden, down_full, up_full, beta_t, bias, rate, q, k, v, go, state)

    end_grad = pl.pallas_call(
        functools.partial(chain_kernel, blocks_ctx),
        out_shape=of_heads(size, size, BF16),
        in_specs=vmem(2),
        out_specs=pl.BlockSpec(memory_space=pltpu.VMEM),
        scratch_shapes=[
            pltpu.VMEM((count, size, size), BF16), pltpu.VMEM((count, size, size), BF16),
            dma((count,)), dma((count,)),
        ],
        compiler_params=remote(1),
        name="state_chain",
    )(maps, adds)

    rows = deep + per_shard * size + (width // size) * count + 2 * count
    unit_rows = 16 * blocks_ctx
    rows = -(-rows // unit_rows) * unit_rows
    dk, dv, dhidden, packed = pl.pallas_call(
        functools.partial(back_kernel, group, shards, steps),
        grid=(steps,),
        out_shape=(
            jax.ShapeDtypeStruct((tokens, count * size), BF16),
            jax.ShapeDtypeStruct((tokens, count * size), BF16),
            jax.ShapeDtypeStruct((tokens, width), BF16),
            jax.ShapeDtypeStruct((shards, rows, size), BF16),
        ),
        in_specs=weights
        + [cols, per_head(size, size), whole(tokens, rank), whole(tokens, count), per_head(size, size)]
        + [square] * 5
        + [per_head(tokens, tokens), square, square],
        out_specs=(cols, cols, whole(tokens, width), whole(shards, rows, size)),
        scratch_shapes=[
            pltpu.VMEM((tokens, rank), F32), pltpu.VMEM((tokens, count), F32),
            pltpu.VMEM((2 * count, size), F32),
        ],
        compiler_params=grid_params,
        name="block_pullback",
    )(hidden, down_full, up_full, beta_t, bias, rate, k, state, low, gates, end_grad,
      cum, wa, wb, u, r, kk, dcum, dkm)

    piece = rows // blocks_ctx
    summed = pl.pallas_call(
        functools.partial(reduce_kernel, shards, blocks_ctx),
        out_shape=jax.ShapeDtypeStruct((rows, size), F32),
        in_specs=vmem(1),
        out_specs=pl.BlockSpec(memory_space=pltpu.VMEM),
        scratch_shapes=[
            pltpu.VMEM((chips, rows, size), BF16), pltpu.VMEM((chips, rows, size), BF16),
            pltpu.VMEM((max(chips - 1, 1), rows, size), BF16), pltpu.VMEM((rows, size), BF16),
            pltpu.VMEM((blocks_ctx - 1, piece, size), BF16), pltpu.VMEM((piece, size), BF16),
            pltpu.VMEM((blocks_ctx - 1, piece, size), BF16),
            dma((chips,)), dma((chips,)), dma((max(chips - 1, 1),)), dma((max(chips - 1, 1),)),
            dma((blocks_ctx - 1,)), dma((blocks_ctx - 1,)),
            dma((blocks_ctx - 1,)), dma((blocks_ctx - 1,)),
        ],
        compiler_params=remote(2),
        name="reduce_weights",
    )(packed)

    up_at = deep + per_shard * size
    beta_at = up_at + (width // size) * count
    up_grad = summed[deep:up_at].reshape(per_shard, rank, size).swapaxes(0, 1).reshape(rank, -1)
    beta_rows = summed[up_at:beta_at].reshape(width // size, count, size)
    beta_full = beta_rows.swapaxes(1, 2).reshape(width, count)
    beta_grad = lax.dynamic_slice_in_dim(beta_full, lax.axis_index("fsdp") * deep, deep, 0)
    vectors = summed[beta_at : beta_at + 2 * count].reshape(2, count * size)
    return (
        dq[None], dk[None], dv[None], dhidden[None],
        summed[:deep], up_grad, beta_grad, vectors[0], vectors[1],
    )


def solution(mesh):
    shards, blocks_ctx = mesh.shape["fsdp"], mesh.shape["ctx"]
    tokens, state = P("fsdp", "ctx", None), P("fsdp", "ctx", None, None, None)
    by_row, by_col = P("fsdp", None), P(None, "fsdp")
    return jax.shard_map(
        functools.partial(on_device, shards, blocks_ctx),
        mesh=mesh,
        in_specs=(tokens,) * 5 + (state, by_row, by_col, P(), P(), by_row),
        out_specs=(tokens,) * 4 + (by_row, by_col, by_row, P(), P()),
        check_vma=False,
    )
```

time: 758 us -> 126 us (0.17)
  waiting for transfers between devices: 274 us -> 0 us
  other arithmetic: 196 us -> 0 us
  Pallas kernels: 0 us -> 107 us
  blocking collectives: 99.9 us -> 0 us
  matrix products: 91.4 us -> 0 us
  local copies, waits for them, and re-layouts: 72.1 us -> 16.1 us
  between operations: 15.2 us -> 0.82 us
    all_gather x2 -> x0, waiting for transfers between devices: 211 us -> none  [carried_in(): pieces = jax.tree.map(lambda part: lax.all_gather(part, axis), value)]
    another operation x8 -> x0, other arithmetic: 191 us -> none  [the longest x5 163 us: block_advance(): jax.scipy.linalg.solve_triangular(system, target, lower=True, unit_diagon...]
    pallas_call x0 -> x5, Pallas kernels: none -> 107 us  [the longest x1 36.1 us: on_device(): pl.pallas_call(functools.partial(chain_kernel, blocks_ctx), out_shape=of_...]
    dot_general x35 -> x0, matrix products: 80.5 us -> none  [the longest x7 26.7 us: combine(): jnp.einsum('hba,hbc->hac', second_map, first_sum, precision=PRECISE)]
    psum x2 -> x0, blocking collectives: 78.1 us -> none  [the longest x1 39.4 us: on_device(): vectors = lax.psum((bias_term, rate_term), ('fsdp', 'ctx'))]
    reduce_scatter x1 -> x0, waiting for transfers between devices: 25.6 us -> none  [on_device(): lax.psum_scatter(up_term, 'fsdp', scatter_dimension=1, tiled=True)]
    all_gather x3 -> x0, blocking collectives: 21.8 us -> none  [the longest x1 9.09 us: on_device(): lax.all_gather(gate_down, 'fsdp', axis=0, tiled=True)]
    unnamed x8 -> x0, waiting for transfers between devices: 19.9 us -> none
  transfers between devices with their start and end apart: 6 -> 0, of which waited for: 5 -> 0; matrix products, arithmetic and copies ran while one was open for 7% -> 0% of each run, Pallas kernels for 0% -> 0%
where the time goes in v1:
time: 126 us; the launch traced here: 124 us
  Pallas kernels  107 us (85%)
  local copies, waits for them, and re-layouts  16.1 us (13%)
    pallas_call x1, Pallas kernels, on_device(): pl.pallas_call(functools.partial(chain_kernel, blocks_ctx), out_shape=of_...  36.1 us
    pallas_call x1, Pallas kernels, on_device(): pl.pallas_call(functools.partial(reduce_kernel, shards, blocks_ctx), out_...  28.3 us
    pallas_call x1, Pallas kernels, on_device(): pl.pallas_call(functools.partial(local_kernel, group), grid=(steps,), out...  19.3 us
    unnamed x37, local copies, waits for them, and re-layouts  13.2 us
    pallas_call x1, Pallas kernels, on_device(): pl.pallas_call(functools.partial(back_kernel, group, shards, steps), grid...  11.7 us
    pallas_call x1, Pallas kernels, on_device(): pl.pallas_call(functools.partial(gather_kernel, shards), out_shape=(jax.S...  11.7 us

profile of v1, /device:TPU:0, one launch (start us, length us, event | category | flops | bytes accessed | tf_op | source)
XLA Modules:
  0.0 124.1 jit_solution(4243143831467087354)
XLA Ops:
  0.6 0.0 copy-start.11
  0.7 0.9 copy-done.11
  1.6 0.9 copy-done.12
  2.5 0.7 copy-done.17
  3.2 11.7 %gather_weights.1 = (bf16[4,576,128]{2,1,0:T(8,128)(2,1)S(1)}, bf16[4,4,128,128]{3,2,1,0:T(8,128)(2,1)S(1)}, bf16[4,16,576]{2,1,0:T(8,128)(2,1)S(1)}) custom-call(bf16[576,128]{1,0:T(8,128)(2,1)S(1)} %copy-done.11, bf16[128,512]{1,0:T(8,128)(2,1)S(1)} %copy-done.12, bf16[16,576]{1,0:T(8,128)(2,1)S(1)} %bitcast.53), custom_call_target="tpu_custom_call" | custom-call | tf_op jit(solution)/shard_map/gather_weights/pallas_call | solution.py:515
  14.9 0.1 reshape.52.beta_t
  15.1 0.0 copy-start.1
  15.1 1.1 copy-done.1
  16.1 1.0 copy-done.3
  17.2 1.0 copy-done.8
  18.2 1.0 copy-done.9
  19.3 1.0 copy-done.10
  20.3 0.7 copy-done.13
  21.0 0.7 copy-done.15
  21.7 19.3 %local_terms.1 = (bf16[128,128]{1,0:T(8,128)(2,1)S(1)}, f32[128,16]{1,0:T(8,128)S(1)}, bf16[128,2048]{1,0:T(8,128)(2,1)}, f32[16,128,128]{2,1,0:T(8,128)S(1)}, b...) custom-call(bf16[128,2304]{1,0:T(8,128)(2,1)S(1)} %bitcast.37, ...), custom_call_target="tpu_custom_call" | custom-call | tf_op jit(solution)/shard_map/local_terms/pallas_call | solution.py:546
  41.0 0.0 copy-start
  41.0 0.0 copy-start.2
  41.0 0.0 copy-start.4
  41.0 0.0 copy-start.6
  41.0 1.4 %copy-done.6 = f32[16,128,128]{2,1,0:T(8,128)S(1)} copy-done((f32[16,128,128]{2,1,0:T(8,128)S(1)}, f32[16,128,128]{2,1,0:T(8,128)}, u32[]{:S(2)}) %copy-start.6) | copy-done | bytes 1048600
  42.4 1.2 copy-done.7
  43.6 36.1 %state_chain.1.x = bf16[16,128,128]{2,1,0:T(8,128)(2,1)S(1)} custom-call(f32[16,128,128]{2,1,0:T(8,128)S(1)} %copy-done.6, f32[16,128,128]{2,1,0:T(8,128)S(1)} %copy-done.7), custom_call_target="tpu_custom_call" | custom-call | tf_op jit(solution)/shard_map/state_chain/pallas_call | solution.py:568
  79.7 0.0 copy-done.14
  79.8 11.7 %block_pullback.1 = (bf16[128,2048]{1,0:T(8,128)(2,1)}, bf16[128,2048]{1,0:T(8,128)(2,1)}, bf16[128,2304]{1,0:T(8,128)(2,1)}, bf16[4,1408,128]{2,1,0:T(8,128)(2,1)}) custom-call(bf16[128,2304]{1,0:T(8,128)(2,1)S(1)} %bitcast.38, bf16[2304,128]{1,0:T(8,128)(2,1)S(1)} %bitcast.40, bf16[16,128,128]{2,1,0:T(8,128)(2,1)S(1)} %bitcast.44, ...), custom_call_target="tpu_custom_call" | custom-call | tf_op jit(solution)/shard_map/block_pullback/pallas_call | solution.py:584
  91.5 0.0 copy-start.5
  91.5 1.4 %copy-done.5 = bf16[4,1408,128]{2,1,0:T(8,128)(2,1)S(1)} copy-done((bf16[4,1408,128]{2,1,0:T(8,128)(2,1)S(1)}, bf16[4,1408,128]{2,1,0:T(8,128)(2,1)}, u32[]{:S(2)}) %copy-start.5) | copy-done | bytes 1441816
  92.9 28.3 %reduce_weights.1 = f32[1408,128]{1,0:T(8,128)S(1)} custom-call(bf16[4,1408,128]{2,1,0:T(8,128)(2,1)S(1)} %copy-done.5), custom_call_target="tpu_custom_call" | custom-call | tf_op jit(solution)/shard_map/reduce_weights/pallas_call | solution.py:608
  121.2 0.7 slice.20
  122.0 0.7 copy.30
  122.7 0.1 copy.25
  122.8 0.7 constant_dynamic-slice_fusion
  123.5 0.6 slice_bitcast_fusion
  (19 shorter events, 0.1 us)
Async XLA Ops:
  0.6 0.9 copy-start.11
  1.6 0.9 copy-start.12
  2.5 0.7 copy-start.17
  15.1 1.1 copy-start.1
  16.1 1.0 copy-start.3
  17.2 1.0 copy-start.8
  18.2 1.0 copy-start.9
  19.3 1.0 copy-start.10
  20.3 0.7 copy-start.13
  21.0 0.7 copy-start.15
  21.7 58.0 %copy-start.14 = (f32[2048]{0:T(1024)S(1)}, f32[2048]{0:T(1024)}, u32[]{:S(2)}) copy-start(f32[2048]{0:T(1024)} %param.19) | copy-start | bytes 24580
  21.7 58.0 %copy-start.16 = (f32[2048]{0:T(1024)S(1)}, f32[2048]{0:T(1024)}, u32[]{:S(2)}) copy-start(f32[2048]{0:T(1024)} %param.20) | copy-start | bytes 24580
  41.0 38.7 %copy-start = (f32[1,1,16,128,128]{4,3,2,1,0:T(8,128)S(1)}, f32[1,1,16,128,128]{4,3,2,1,0:T(8,128)}, u32[]{:S(2)}) copy-start(f32[1,1,16,128,128]{4,3,2,1,0:T(8,128)} %param.16) | copy-start | bytes 3145732
  41.0 38.7 %copy-start.2 = (bf16[1,128,2304]{2,1,0:T(8,128)(2,1)S(1)}, bf16[1,128,2304]{2,1,0:T(8,128)(2,1)}, u32[]{:S(2)}) copy-start(bf16[1,128,2304]{2,1,0:T(8,128)(2,1)} %param.11) | copy-start | bytes 1769476
  41.0 38.7 %copy-start.4 = (bf16[1,128,2048]{2,1,0:T(8,128)(2,1)S(1)}, bf16[1,128,2048]{2,1,0:T(8,128)(2,1)}, u32[]{:S(2)}) copy-start(bf16[1,128,2048]{2,1,0:T(8,128)(2,1)} %param.13) | copy-start | bytes 1572868
  41.0 1.4 %copy-start.6 = (f32[16,128,128]{2,1,0:T(8,128)S(1)}, f32[16,128,128]{2,1,0:T(8,128)}, u32[]{:S(2)}) copy-start(f32[16,128,128]{2,1,0:T(8,128)} %get-tuple-element.35.maps) | copy-start | bytes 3145732
  42.4 1.2 copy-start.7
  91.5 1.4 %copy-start.5 = (bf16[4,1408,128]{2,1,0:T(8,128)(2,1)S(1)}, bf16[4,1408,128]{2,1,0:T(8,128)(2,1)}, u32[]{:S(2)}) copy-start(bf16[4,1408,128]{2,1,0:T(8,128)(2,1)} %get-tuple-element.48.packed) | copy-start | bytes 4325380

commit v2 on v1

v2 whole, which is shorter than its diff:
```python
import functools

import jax
import jax.numpy as jnp
from jax import lax
from jax.experimental import pallas as pl
from jax.experimental.pallas import tpu as pltpu
from jax.sharding import PartitionSpec as P

EPSILON = 1e-06
MESH = pl.DeviceIdType.MESH
F32, BF16 = jnp.float32, jnp.bfloat16
VMEM_LIMIT = 48 * 1024 * 1024
NN, NT, TN = ((1,), (0,)), ((1,), (1,)), ((0,), (0,))
INV_PASSES = 1
PASSES = 3


def dot(left, right, dims=NN):
    return lax.dot_general(left, right, (dims, ((), ())), preferred_element_type=F32)


def halves(value):
    if value.dtype == BF16:
        return value, None
    high = value.astype(BF16)
    return high, (value - high.astype(F32)).astype(BF16)


def mm(left, right, dims=NN, passes=None):
    passes = PASSES if passes is None else passes
    if passes == 1:
        return dot(left.astype(BF16), right.astype(BF16), dims)
    left_high, left_low = halves(left)
    right_high, right_low = halves(right)
    total = dot(left_high, right_high, dims)
    if left_low is not None:
        total += dot(left_low, right_high, dims)
    if right_low is not None:
        total += dot(left_high, right_low, dims)
    return total


def sum_by(ones, value):
    high = value.astype(BF16)
    rest = value - high.astype(F32)
    mid = rest.astype(BF16)
    low = (rest - mid.astype(F32)).astype(BF16)
    return dot(ones, high) + dot(ones, mid) + dot(ones, low)


def iotas(size):
    return (
        lax.broadcasted_iota(jnp.int32, (size, size), 0),
        lax.broadcasted_iota(jnp.int32, (size, size), 1),
    )


def inverse(systems):
    size = systems[0].shape[0]
    row, col = iotas(size)
    eye = jnp.where(row == col, 1.0, 0.0)

    def off(block):
        same = row // (2 * block) == col // (2 * block)
        return same & ((row // block) % 2 == 1) & ((col // block) % 2 == 0)

    found = [eye - jnp.where(off(1), system, 0.0) for system in systems]
    block = 2
    while block < size:
        mask = off(block)
        parts = [mm(jnp.where(mask, s, 0.0), t, NN, INV_PASSES) for s, t in zip(systems, found)]
        found = [t - mm(t, p, NN, INV_PASSES) for t, p in zip(found, parts)]
        block *= 2
    return found


def softplus(value):
    return jnp.maximum(value, 0.0) + jnp.log1p(jnp.exp(-jnp.abs(value)))


def sigmoid(value):
    return 1.0 / (1.0 + jnp.exp(-value))


def unit(rows):
    scale = lax.rsqrt(jnp.sum(rows * rows, axis=-1, keepdims=True) + EPSILON)
    return rows * scale, scale


def unit_back(grad, rows, scale):
    return scale * (grad - rows * jnp.sum(grad * rows, axis=-1, keepdims=True))


def head_terms(keys, gate_in, rate):
    size = keys.shape[0]
    row, col = iotas(size)
    kn, k_scale = unit(keys.astype(F32))
    ones = jnp.where(row >= col, 1.0, 0.0).astype(BF16)
    cumulative = sum_by(ones, -rate * softplus(gate_in))
    return kn, k_scale, cumulative


def first_heads(heads):
    row, col = iotas(heads[0]["k"].shape[0])
    for h in heads:
        kn, _, cum = head_terms(h["k"], h["gate_in"], h["rate"])
        qn, _ = unit(h["q"].astype(F32))
        plus = jnp.exp(cum)
        h.update(cum=cum, kp=kn * plus, km=kn * jnp.exp(-cum), qp=qn * plus)
        h.update(ke=kn * jnp.exp(cum[-1:] - cum))
    for h in heads:
        h["kk"] = jnp.where(row > col, mm(h["kp"], h["km"], NT), 0.0)
        h["p"] = jnp.where(row >= col, mm(h["qp"], h["km"], NT), 0.0)
    for h, t in zip(heads, inverse([h["kk"] * h["beta"] for h in heads])):
        h["t"] = t
    for h in heads:
        h["pg"] = mm(h["p"], h["go"], TN)
    for h in heads:
        h["wa"] = mm(h["t"], h["ke"], TN)
        h["wb"] = mm(h["t"], h["pg"], TN)
    for h in heads:
        kb = h["kp"] * h["beta"]
        end = jnp.exp(h["cum"][-1:])
        h["map"] = jnp.where(row == col, end, 0.0) - mm(kb, h["wa"], TN)
        h["add"] = mm(h["qp"], h["go"], TN) - mm(kb, h["wb"], TN)
    return heads


def rest_heads(heads):
    row, col = iotas(heads[0]["k"].shape[0])
    for h in heads:
        kn, _ = unit(h["k"].astype(F32))
        qn, q_scale = unit(h["q"].astype(F32))
        plus = jnp.exp(h["cum"])
        h.update(plus=plus, qn=qn, q_scale=q_scale)
        h.update(kp=kn * plus, km=kn * jnp.exp(-h["cum"]), qp=qn * plus)
        h["r"] = h["v"].astype(F32) - mm(h["kp"], h["s"])
    for h in heads:
        h["u"] = mm(h["t"], h["beta"] * h["r"])
    for h in heads:
        h["dp"] = jnp.where(row >= col, mm(h["go"], h["u"], NT), 0.0)
    for h in heads:
        dqp = mm(h["go"], h["s"], NT) + mm(h["dp"], h["km"])
        h["dq"] = unit_back(dqp * h["plus"], h["qn"], h["q_scale"])
        h["dcum"] = dqp * h["qp"]
        h["dkm"] = mm(h["dp"], h["qp"], TN)
    return heads


def back_heads(heads):
    size = heads[0]["k"].shape[0]
    row, col = iotas(size)
    ones = jnp.where(row <= col, 1.0, 0.0).astype(BF16)
    for h in heads:
        kn, k_scale = unit(h["k"].astype(F32))
        cum = h["cum"]
        plus, minus, end = jnp.exp(cum), jnp.exp(-cum), jnp.exp(cum[-1:] - cum)
        h.update(kn=kn, k_scale=k_scale, plus=plus, minus=minus, end=end, kp=kn * plus)
        h["w"] = h["wb"] + mm(h["wa"], h["x"])
    for h in heads:
        h["dv"] = h["beta"] * h["w"]
        h["dm"] = jnp.where(row > col, -mm(h["w"], h["u"], NT), 0.0)
        h["dke"] = mm(h["u"], h["x"], NT)
    for h in heads:
        kn = h["kn"]
        km, ke = kn * h["minus"], kn * h["end"]
        dmb = h["beta"] * h["dm"]
        h["dbeta"] = jnp.sum(h["w"] * h["r"] + h["dm"] * h["kk"], axis=1, keepdims=True)
        dkp = mm(dmb, km) - mm(h["dv"], h["s"], NT)
        dkm = mm(dmb, h["kp"], TN) + h["dkm"]
        ended = h["dke"] * ke
        kept = jnp.sum((h["x"] * h["s"]).T, axis=0, keepdims=True) * jnp.exp(h["cum"][-1:])
        last = jnp.sum(ended, axis=0, keepdims=True) + kept
        dcum = h["dcum"] + dkp * h["kp"] - dkm * km - ended
        h["dg"] = sum_by(ones, dcum) + last
        grad = dkp * h["plus"] + dkm * h["minus"] + h["dke"] * h["end"]
        h["dk"] = unit_back(grad, kn, h["k_scale"])
    for h in heads:
        gate = sigmoid(h["gate_in"])
        h["dgate"] = h["dg"] * -h["rate"] * gate
        h["rate_row"] = -jnp.sum(h["dg"] * softplus(h["gate_in"]), axis=0, keepdims=True)
        h["bias_row"] = jnp.sum(h["dgate"], axis=0, keepdims=True)
    return heads


def column(table, index):
    lanes = lax.broadcasted_iota(jnp.int32, table.shape, 1)
    return jnp.sum(jnp.where(lanes == index, table, 0.0), axis=1, keepdims=True)


def fused_kernel(
    shards, count_ctx, group,
    hidden_in, q_in, k_in, v_in, go_in, s_in, down_in, up_in, beta_in, bias, rate,
    dq_out, dk_out, dv_out, dhidden_out, out,
    hidden, q, k, v, go, s, dq, dk, dv, dhidden, down_all, up_all, beta_all, beta_full,
    low, gates, cum, t, wa, wb, u, r, kk, dcum, dkm, maps, adds, sent, got,
    low_sum, beta_cot, rows, packed,
    core_got, core_sum, chip_got, chip_sum, piece_got, total, spread,
    load_sem, store_sem, gather_send, gather_recv, chain_send, chain_recv,
    core_send, core_recv, chip_send, chip_recv, piece_send, piece_recv, spread_send, spread_recv,
):
    me, mine = lax.axis_index("fsdp"), lax.axis_index("ctx")
    chips = shards // 2
    chip, core = me // 2, me % 2
    sibling = chip * 2 + (1 - core)
    peers = [lax.rem(chip + d, chips) * 2 + core for d in range(1, chips)]
    sources = [lax.rem(chip + chips - d, chips) * 2 + core for d in range(1, chips)]
    piece = packed.shape[1] // count_ctx
    count, size = s.shape[0], s.shape[-1]
    groups = count // group
    per_shard = count // shards
    deep = down_all.shape[1]
    first_rep = deep + per_shard * size

    loads = [
        pltpu.make_async_copy(src, dst, load_sem.at[i])
        for i, (src, dst) in enumerate(
            ((hidden_in, hidden), (k_in, k), (q_in, q), (go_in, go), (s_in, s), (v_in, v))
        )
    ]
    for c in loads:
        c.start()
    barrier = pltpu.get_barrier_semaphore()
    for other in [sibling] + peers:
        pl.semaphore_signal(barrier, inc=1, device_id={"fsdp": other}, device_id_type=MESH)

    def greet(d, _):
        pl.semaphore_signal(
            barrier, inc=1, device_id={"ctx": lax.rem(mine + d, count_ctx)}, device_id_type=MESH
        )
        return 0

    lax.fori_loop(1, count_ctx, greet, 0)
    for i in range(per_shard):
        up_all[me, i] = up_in[:, i * size : (i + 1) * size]
    down_all[me] = down_in[...]
    beta_all[me] = beta_in[...]
    low_sum[...] = jnp.zeros_like(low_sum)
    beta_cot[...] = jnp.zeros_like(beta_cot)

    @pl.when(mine == count_ctx - 1)
    def _():
        got[...] = jnp.zeros_like(got)

    pl.semaphore_wait(barrier, chips + count_ctx - 1)

    def copies(shard, target, slot):
        return [
            pltpu.make_async_remote_copy(
                src_ref=ref.at[shard], dst_ref=ref.at[shard],
                send_sem=gather_send.at[slot, i], recv_sem=gather_recv.at[slot, i],
                device_id={"fsdp": target}, device_id_type=MESH,
            )
            for i, ref in enumerate((down_all, beta_all, up_all))
        ]

    for d, peer in enumerate(peers):
        for c in copies(me, peer, 1 + d):
            c.start()
    for c in copies(me, sibling, 0):
        c.start()
    for d, source in enumerate(sources):
        for c, onward in zip(copies(source, peers[d], 1 + d), copies(source, sibling, chips + d)):
            c.wait_recv()
            onward.start()
    for c in copies(sibling, sibling, 0):
        c.wait_recv()
    for d, source in enumerate(sources):
        theirs = (source // 2) * 2 + (1 - core)
        for c in copies(theirs, sibling, chips + d):
            c.wait_recv()
    for c in loads:
        c.wait()

    for shard in range(shards):
        turned = beta_all[shard].astype(F32).T
        beta_full[shard * deep : (shard + 1) * deep, :] = turned[:deep].astype(BF16)
    low[...] = dot(hidden[...], down_all[...].reshape(shards * deep, -1)).astype(BF16)
    gates[...] = sigmoid(dot(hidden[...], beta_full[...]))

    def chain_copy(head):
        return pltpu.make_async_remote_copy(
            src_ref=sent.at[head], dst_ref=got.at[head],
            send_sem=chain_send.at[head], recv_sem=chain_recv.at[head],
            device_id={"ctx": jnp.maximum(mine - 1, 0)}, device_id_type=MESH,
        )

    hop = count_ctx - 1 - mine
    late = jnp.minimum(groups + 1 + 2 * (hop - groups), 2 * groups - 1)
    first_slot = jnp.where(hop < groups, hop, late)

    def chain_turn(head, _):
        @pl.when(mine < count_ctx - 1)
        def _():
            chain_copy(head).wait_recv()

        @pl.when(mine > 0)
        def _():
            sent[head] = (adds[head] + mm(maps[head], got[head], NN, 3)).astype(BF16)
            chain_copy(head).start()

        return 0

    def chain(slot):
        part = slot - first_slot

        @pl.when((part >= 0) & (part < groups))
        def _():
            lax.fori_loop(part * group, part * group + group, chain_turn, 0)

    def take(g, i):
        head = g * group + i
        at = pl.ds(pl.multiple_of(head * size, size), size)
        return head, at, dict(rate=rate[:, at], beta=column(gates[...], head))

    def gate_in(head, at):
        return dot(low[...], up_all[head // per_shard, head % per_shard]) + bias[:, at]

    def first(g, _):
        heads = []
        for i in range(group):
            head, at, h = take(g, i)
            h.update(q=q[:, at], k=k[:, at], go=go[:, at], gate_in=gate_in(head, at))
            heads.append(h)
        for i, h in enumerate(first_heads(heads)):
            n = g * group + i
            cum[n], kk[n], t[n], wa[n], wb[n] = h["cum"], h["kk"], h["t"], h["wa"].astype(BF16), h["wb"]
            maps[n], adds[n] = h["map"], h["add"]
        chain(g)
        return 0

    def rest(g, _):
        heads = []
        for i in range(group):
            head, at, h = take(g, i)
            h.update(q=q[:, at], k=k[:, at], v=v[:, at], go=go[:, at])
            h.update(s=s[head], cum=cum[head], t=t[head])
            heads.append(h)
        for i, h in enumerate(rest_heads(heads)):
            n, at, _ = take(g, i)
            dq[:, at] = h["dq"].astype(BF16)
            u[n], r[n], dcum[n], dkm[n] = h["u"].astype(BF16), h["r"], h["dcum"], h["dkm"]
        chain(groups + g)
        return 0

    lanes = lax.broadcasted_iota(jnp.int32, beta_cot.shape, 1)

    def back(g, _):
        heads = []
        for i in range(group):
            n, at, h = take(g, i)
            h.update(k=k[:, at], s=s[n], x=got[n].astype(F32), gate_in=gate_in(n, at))
            h.update(cum=cum[n], wa=wa[n], wb=wb[n], u=u[n], r=r[n], kk=kk[n], dcum=dcum[n], dkm=dkm[n])
            heads.append(h)
        for i, h in enumerate(back_heads(heads)):
            head, at, _ = take(g, i)
            dk[:, at] = h["dk"].astype(BF16)
            dv[:, at] = h["dv"].astype(BF16)
            half = h["dgate"].astype(BF16)
            place = pl.multiple_of(deep + (head % per_shard) * size, 16)
            packed[head // per_shard, pl.ds(place, size), :] = dot(low[...], half, TN).astype(BF16)
            low_sum[...] += dot(half, up_all[head // per_shard, head % per_shard], NT)
            beta_cot[...] += jnp.where(lanes == head, h["dbeta"], 0.0)
            rows[pl.ds(head, 1), :] = h["bias_row"]
            rows[pl.ds(count + head, 1), :] = h["rate_row"]
        chain(2 * groups + g)
        return 0

    stores = [
        pltpu.make_async_copy(src, dst, store_sem.at[i])
        for i, (src, dst) in enumerate(
            ((dq, dq_out), (dk, dk_out), (dv, dv_out), (dhidden, dhidden_out))
        )
    ]
    lax.fori_loop(0, groups, first, 0)
    lax.fori_loop(0, groups, rest, 0)
    stores[0].start()
    lax.fori_loop(0, groups, back, 0)
    stores[1].start()
    stores[2].start()

    low_grad = low_sum[...].astype(BF16)
    gate = gates[...]
    score = (beta_cot[...] * gate * (1.0 - gate)).astype(BF16)
    down_term = dot(hidden[...], low_grad, TN).astype(BF16)
    beta_term = dot(score, hidden[...], TN).astype(BF16)
    tail = rows[...].astype(BF16)
    blocks = hidden.shape[1] // size
    for shard in range(shards):
        packed[shard, :deep, :] = down_term[shard * deep : (shard + 1) * deep]
        for b in range(blocks):
            place = first_rep + b * count
            packed[shard, place : place + count, :] = beta_term[:, b * size : (b + 1) * size]
        place = first_rep + blocks * count
        packed[shard, place : place + 2 * count, :] = tail
        if place + 2 * count < packed.shape[1]:
            left = packed.shape[1] - place - 2 * count
            packed[shard, place + 2 * count :, :] = jnp.zeros((left, packed.shape[2]), BF16)

    def core_copy(c):
        return pltpu.make_async_remote_copy(
            src_ref=packed.at[c * 2 + (1 - core)], dst_ref=core_got.at[c],
            send_sem=core_send.at[c], recv_sem=core_recv.at[c],
            device_id={"fsdp": sibling}, device_id_type=MESH,
        )

    def chip_copy(d, peer):
        return pltpu.make_async_remote_copy(
            src_ref=core_sum.at[peer // 2], dst_ref=chip_got.at[d],
            send_sem=chip_send.at[d], recv_sem=chip_recv.at[d],
            device_id={"fsdp": peer}, device_id_type=MESH,
        )

    order = [peer // 2 for peer in peers] + [chip]
    for c in order:
        core_copy(c).start()
    dhidden[...] = (
        dot(low_grad, down_all[...].reshape(shards * deep, -1), NT) + dot(score, beta_full[...], NT)
    ).astype(BF16)
    stores[3].start()
    for d, c in enumerate(order):
        core_copy(c).wait_recv()
        both = packed[c * 2 + core].astype(F32) + core_got[c].astype(F32)
        if d < chips - 1:
            core_sum[c] = both.astype(BF16)
            chip_copy(d, peers[d]).start()
        else:
            own = both
    for d in range(chips - 1):
        chip_copy(d, peers[d]).wait_recv()
        own = own + chip_got[d].astype(F32)
    chip_sum[...] = own.astype(BF16)

    def piece_copy(d):
        other = lax.rem(mine + d, count_ctx)
        at = pl.multiple_of(other * piece, 16)
        return pltpu.make_async_remote_copy(
            src_ref=chip_sum.at[pl.ds(at, piece)], dst_ref=piece_got.at[d - 1],
            send_sem=piece_send.at[d - 1], recv_sem=piece_recv.at[d - 1],
            device_id={"ctx": other}, device_id_type=MESH,
        )

    def spread_copy(d):
        return pltpu.make_async_remote_copy(
            src_ref=total, dst_ref=spread.at[d - 1],
            send_sem=spread_send.at[d - 1], recv_sem=spread_recv.at[d - 1],
            device_id={"ctx": lax.rem(mine + d, count_ctx)}, device_id_type=MESH,
        )

    def start_piece(d, _):
        piece_copy(d).start()
        return 0

    def add_piece(d, so_far):
        piece_copy(d).wait_recv()
        return so_far + piece_got[d - 1].astype(F32)

    def start_spread(d, _):
        spread_copy(d).start()
        return 0

    def place_spread(d, _):
        spread_copy(d).wait_recv()
        source = lax.rem(mine + count_ctx - d, count_ctx)
        out[pl.ds(pl.multiple_of(source * piece, 16), piece), :] = spread[d - 1].astype(F32)
        return 0

    def finish(d, _):
        piece_copy(d).wait_send()
        spread_copy(d).wait_send()
        return 0

    lax.fori_loop(1, count_ctx, start_piece, 0)
    at = pl.multiple_of(mine * piece, 16)
    summed = lax.fori_loop(1, count_ctx, add_piece, chip_sum[pl.ds(at, piece), :].astype(F32))
    total[...] = summed.astype(BF16)
    lax.fori_loop(1, count_ctx, start_spread, 0)
    out[pl.ds(at, piece), :] = total[...].astype(F32)
    lax.fori_loop(1, count_ctx, place_spread, 0)
    lax.fori_loop(1, count_ctx, finish, 0)
    for c in range(chips):
        core_copy(c).wait_send()
    for d, peer in enumerate(peers):
        chip_copy(d, peer).wait_send()
    for slot in range(2 * chips - 1):
        for c in copies(me, sibling, slot):
            c.wait_send()

    @pl.when(mine > 0)
    def _():
        def done(head, _):
            chain_copy(head).wait_send()
            return 0

        lax.fori_loop(0, count, done, 0)

    for c in stores:
        c.wait()


def vmem(count):
    return [pl.BlockSpec(memory_space=pltpu.VMEM)] * count


def remote(collective):
    return pltpu.CompilerParams(
        collective_id=collective, has_side_effects=True, vmem_limit_bytes=VMEM_LIMIT
    )


def on_device(
    shards, blocks_ctx,
    hidden, query_heads, key_heads, value_heads, out_grad, checkpoint,
    gate_down, gate_up, gate_bias, decay_rate, beta_weight,
):
    tokens, width = hidden.shape[1], hidden.shape[2]
    count, size = checkpoint.shape[2], checkpoint.shape[3]
    rank = gate_down.shape[1]
    deep = gate_down.shape[0]
    per_shard = count // shards
    chips = shards // 2
    hidden, q, k, v, go = (a[0] for a in (hidden, query_heads, key_heads, value_heads, out_grad))
    state = checkpoint[0, 0]
    bias, rate = gate_bias.reshape(1, -1), decay_rate.reshape(1, -1)
    dma = pltpu.SemaphoreType.DMA

    group = 4 if count % 4 == 0 else 1
    rows = deep + per_shard * size + (width // size) * count + 2 * count
    unit_size = 16 * blocks_ctx
    rows = -(-rows // unit_size) * unit_size
    piece = rows // blocks_ctx
    far = max(chips - 1, 1)
    wide = -(-deep // size) * size
    beta_t = jnp.pad(beta_weight.T, ((0, 0), (0, wide - deep)))
    channels = count * size
    anywhere = pl.BlockSpec(memory_space=pl.ANY)
    heads_f32 = pltpu.VMEM((count, tokens, size), F32)
    heads_bf16 = pltpu.VMEM((count, tokens, size), BF16)
    states_f32 = pltpu.VMEM((count, size, size), F32)
    states_bf16 = pltpu.VMEM((count, size, size), BF16)
    mixed = pltpu.VMEM((count, tokens, tokens), F32)
    sided = pltpu.VMEM((tokens, channels), BF16)
    sized = pltpu.VMEM((tokens, width), BF16)
    dq, dk, dv, dhidden, summed = pl.pallas_call(
        functools.partial(fused_kernel, shards, blocks_ctx, group),
        out_shape=(
            jax.ShapeDtypeStruct((tokens, channels), BF16),
            jax.ShapeDtypeStruct((tokens, channels), BF16),
            jax.ShapeDtypeStruct((tokens, channels), BF16),
            jax.ShapeDtypeStruct((tokens, width), BF16),
            jax.ShapeDtypeStruct((rows, size), F32),
        ),
        in_specs=[anywhere] * 6 + vmem(5),
        out_specs=(anywhere,) * 4 + (pl.BlockSpec(memory_space=pltpu.VMEM),),
        scratch_shapes=[
            sized, sided, sided, sided, sided, states_f32, sided, sided, sided, sized,
            pltpu.VMEM((shards, deep, rank), BF16),
            pltpu.VMEM((shards, per_shard, rank, size), BF16),
            pltpu.VMEM((shards, count, wide), BF16), pltpu.VMEM((width, count), BF16),
            pltpu.VMEM((tokens, rank), BF16), pltpu.VMEM((tokens, count), F32),
            heads_f32, mixed, heads_bf16, heads_f32, heads_bf16, heads_f32, mixed, heads_f32, heads_f32,
            states_f32, states_f32, states_bf16, states_bf16,
            pltpu.VMEM((tokens, rank), F32), pltpu.VMEM((tokens, count), F32),
            pltpu.VMEM((2 * count, size), F32), pltpu.VMEM((shards, rows, size), BF16),
            pltpu.VMEM((chips, rows, size), BF16), pltpu.VMEM((chips, rows, size), BF16),
            pltpu.VMEM((far, rows, size), BF16), pltpu.VMEM((rows, size), BF16),
            pltpu.VMEM((blocks_ctx - 1, piece, size), BF16), pltpu.VMEM((piece, size), BF16),
            pltpu.VMEM((blocks_ctx - 1, piece, size), BF16),
            dma((6,)), dma((4,)), dma((2 * chips - 1, 3)), dma((2 * chips - 1, 3)),
            dma((count,)), dma((count,)),
            dma((chips,)), dma((chips,)), dma((far,)), dma((far,)),
            dma((blocks_ctx - 1,)), dma((blocks_ctx - 1,)),
            dma((blocks_ctx - 1,)), dma((blocks_ctx - 1,)),
        ],
        compiler_params=remote(0),
        name="delta_backward",
    )(hidden, q, k, v, go, state, gate_down, gate_up, beta_t, bias, rate)

    up_at = deep + per_shard * size
    beta_at = up_at + (width // size) * count
    up_grad = summed[deep:up_at].reshape(per_shard, rank, size).swapaxes(0, 1).reshape(rank, -1)
    beta_rows = summed[up_at:beta_at].reshape(width // size, count, size)
    beta_full = beta_rows.swapaxes(1, 2).reshape(width, count)
    beta_grad = lax.dynamic_slice_in_dim(beta_full, lax.axis_index("fsdp") * deep, deep, 0)
    vectors = summed[beta_at : beta_at + 2 * count].reshape(2, count * size)
    return (
        dq[None], dk[None], dv[None], dhidden[None],
        summed[:deep], up_grad, beta_grad, vectors[0], vectors[1],
    )


def solution(mesh):
    shards, blocks_ctx = mesh.shape["fsdp"], mesh.shape["ctx"]
    tokens, state = P("fsdp", "ctx", None), P("fsdp", "ctx", None, None, None)
    by_row, by_col = P("fsdp", None), P(None, "fsdp")
    return jax.shard_map(
        functools.partial(on_device, shards, blocks_ctx),
        mesh=mesh,
        in_specs=(tokens,) * 5 + (state, by_row, by_col, P(), P(), by_row),
        out_specs=(tokens,) * 4 + (by_row, by_col, by_row, P(), P()),
        check_vma=False,
    )
```

time: 126 us -> 100 us (0.79); the launches traced: 124 us -> 99.7 us
  Pallas kernels: 107 us -> 84.4 us
  local copies, waits for them, and re-layouts: 16.1 us -> 14.5 us
    pallas_call x5 -> x1, Pallas kernels: 107 us -> 84.4 us  [on_device(): pl.pallas_call(functools.partial(fused_kernel, shards, blocks_ctx, group)...]
    unnamed x37 -> x25, local copies, waits for them, and re-layouts: 13.2 us -> 11.7 us
where the time goes in v2:
time: 100 us; the launch traced here: 99.7 us
  Pallas kernels  84.4 us (84%)
  local copies, waits for them, and re-layouts  14.5 us (14%)
    pallas_call x1, Pallas kernels, on_device(): pl.pallas_call(functools.partial(fused_kernel, shards, blocks_ctx, group)...  84.4 us
    unnamed x25, local copies, waits for them, and re-layouts  11.7 us

profile of v2, /device:TPU:0, one launch (start us, length us, event | category | flops | bytes accessed | tf_op | source)
XLA Modules:
  0.0 99.7 jit_solution(12721545154627143938)
XLA Ops:
  0.6 0.0 copy-start.9
  0.7 0.7 copy-done.9
  1.4 0.0 copy-start.7
  1.4 0.0 copy-start.8
  1.4 0.7 copy-done.7
  2.1 0.0 copy-done.8
  2.1 0.0 copy-start
  2.1 1.1 %copy-done = bf16[1,128,2304]{2,1,0:T(8,128)(2,1)S(1)} copy-done((bf16[1,128,2304]{2,1,0:T(8,128)(2,1)S(1)}, bf16[1,128,2304]{2,1,0:T(8,128)(2,1)}, u32[]{:S(2)}) %copy-start) | copy-done | bytes 589848
  3.2 0.0 copy-start.1
  3.2 1.0 %copy-done.1 = bf16[1,128,2048]{2,1,0:T(8,128)(2,1)S(1)} copy-done((bf16[1,128,2048]{2,1,0:T(8,128)(2,1)S(1)}, bf16[1,128,2048]{2,1,0:T(8,128)(2,1)}, u32[]{:S(2)}) %copy-start.1) | copy-done | bytes 524312
  4.2 0.0 copy-start.2
  4.2 1.0 %copy-done.2 = bf16[1,128,2048]{2,1,0:T(8,128)(2,1)S(1)} copy-done((bf16[1,128,2048]{2,1,0:T(8,128)(2,1)S(1)}, bf16[1,128,2048]{2,1,0:T(8,128)(2,1)}, u32[]{:S(2)}) %copy-start.2) | copy-done | bytes 524312
  5.2 0.0 copy-start.3
  5.2 1.0 %copy-done.3 = bf16[1,128,2048]{2,1,0:T(8,128)(2,1)S(1)} copy-done((bf16[1,128,2048]{2,1,0:T(8,128)(2,1)S(1)}, bf16[1,128,2048]{2,1,0:T(8,128)(2,1)}, u32[]{:S(2)}) %copy-start.3) | copy-done | bytes 524312
  6.3 0.0 copy-start.4
  6.3 1.0 %copy-done.4 = bf16[1,128,2048]{2,1,0:T(8,128)(2,1)S(1)} copy-done((bf16[1,128,2048]{2,1,0:T(8,128)(2,1)S(1)}, bf16[1,128,2048]{2,1,0:T(8,128)(2,1)}, u32[]{:S(2)}) %copy-start.4) | copy-done | bytes 524312
  7.3 0.0 copy-start.5
  7.3 0.9 copy-done.5
  8.2 0.0 copy-start.6
  8.2 0.9 copy-done.6
  9.1 84.4 %delta_backward.1 = (bf16[128,2048]{1,0:T(8,128)(2,1)S(1)}, bf16[128,2048]{1,0:T(8,128)(2,1)S(1)}, bf16[128,2048]{1,0:T(8,128)(2,1)S(1)}, bf16[128,2304]{1,0:T(8,128)(2,1)S(1)}, f32[1408,128]{1,0:T(8,128)S(1)}) custom-call(bf16[128,2304]{1,0:T(8,128)(2,1)S(1)} %bitcast.32, bf16[128,2048]{1,0:T(8,128)(2,1)S(1)} %bitcast.34, bf16[128,2048]{1,0:T(8,128)(2,1)S(1)} %bitcast.35, ...), custom_call_target="tpu_custom_call" | custom-call | tf_op jit(solution)/shard_map/delta_backward/pallas_call | solution.py:545
  93.5 0.6 slice_bitcast_fusion
  94.2 0.1 copy.23
  94.3 0.7 constant_dynamic-slice_fusion
  95.0 0.7 slice.20
  95.7 0.7 copy.28
  96.5 0.8 copy.34
  97.2 0.8 copy.35
  98.0 0.8 copy.36
  98.8 0.8 copy.37
  (4 shorter events, 0.1 us)
Async XLA Ops:
  0.6 0.7 copy-start.9
  1.4 0.7 copy-start.7
  1.4 0.7 copy-start.8
  2.1 1.1 %copy-start = (bf16[1,128,2304]{2,1,0:T(8,128)(2,1)S(1)}, bf16[1,128,2304]{2,1,0:T(8,128)(2,1)}, u32[]{:S(2)}) copy-start(bf16[1,128,2304]{2,1,0:T(8,128)(2,1)} %param.11) | copy-start | bytes 1769476
  3.2 1.0 %copy-start.1 = (bf16[1,128,2048]{2,1,0:T(8,128)(2,1)S(1)}, bf16[1,128,2048]{2,1,0:T(8,128)(2,1)}, u32[]{:S(2)}) copy-start(bf16[1,128,2048]{2,1,0:T(8,128)(2,1)} %param.12) | copy-start | bytes 1572868
  4.2 1.0 %copy-start.2 = (bf16[1,128,2048]{2,1,0:T(8,128)(2,1)S(1)}, bf16[1,128,2048]{2,1,0:T(8,128)(2,1)}, u32[]{:S(2)}) copy-start(bf16[1,128,2048]{2,1,0:T(8,128)(2,1)} %param.13) | copy-start | bytes 1572868
  5.2 1.0 %copy-start.3 = (bf16[1,128,2048]{2,1,0:T(8,128)(2,1)S(1)}, bf16[1,128,2048]{2,1,0:T(8,128)(2,1)}, u32[]{:S(2)}) copy-start(bf16[1,128,2048]{2,1,0:T(8,128)(2,1)} %param.14) | copy-start | bytes 1572868
  6.3 1.0 %copy-start.4 = (bf16[1,128,2048]{2,1,0:T(8,128)(2,1)S(1)}, bf16[1,128,2048]{2,1,0:T(8,128)(2,1)}, u32[]{:S(2)}) copy-start(bf16[1,128,2048]{2,1,0:T(8,128)(2,1)} %param.15) | copy-start | bytes 1572868
  7.3 0.9 copy-start.5
  8.2 0.9 copy-start.6

commit v3 on v2

--- a/solution.py
+++ b/solution.py
@@ -10,7 +10,7 @@
 EPSILON = 1e-06
 MESH = pl.DeviceIdType.MESH
 F32, BF16 = jnp.float32, jnp.bfloat16
-VMEM_LIMIT = 48 * 1024 * 1024
+VMEM_LIMIT = 60 * 1024 * 1024
 NN, NT, TN = ((1,), (0,)), ((1,), (1,)), ((0,), (0,))
 INV_PASSES = 1
 PASSES = 3
@@ -33,12 +33,14 @@
         return dot(left.astype(BF16), right.astype(BF16), dims)
     left_high, left_low = halves(left)
     right_high, right_low = halves(right)
-    total = dot(left_high, right_high, dims)
+    lefts, rights = [left_high], [right_high]
     if left_low is not None:
-        total += dot(left_low, right_high, dims)
+        lefts, rights = lefts + [left_low], rights + [right_high]
     if right_low is not None:
-        total += dot(left_high, right_low, dims)
-    return total
+        lefts, rights = lefts + [left_high], rights + [right_low]
+    return dot(
+        jnp.concatenate(lefts, axis=dims[0][0]), jnp.concatenate(rights, axis=dims[1][0]), dims
+    )
 
 
 def sum_by(ones, value):
@@ -46,7 +48,7 @@
     rest = value - high.astype(F32)
     mid = rest.astype(BF16)
     low = (rest - mid.astype(F32)).astype(BF16)
-    return dot(ones, high) + dot(ones, mid) + dot(ones, low)
+    return dot(jnp.concatenate([ones] * 3, axis=1), jnp.concatenate([high, mid, low], axis=0))
 
 
 def iotas(size):
@@ -191,9 +193,9 @@
 
 def fused_kernel(
     shards, count_ctx, group,
-    hidden_in, q_in, k_in, v_in, go_in, s_in, down_in, up_in, beta_in, bias, rate,
+    hidden_in, q_in, k_in, v_in, go_in, s_in, down_in, up_in, beta_in, bias_in, rate_in,
     dq_out, dk_out, dv_out, dhidden_out, out,
-    hidden, q, k, v, go, s, dq, dk, dv, dhidden, down_all, up_all, beta_all, beta_full,
+    bias, rate, hidden, q, k, v, go, s, dq, dk, dv, dhidden, down_all, up_all, beta_all, beta_full,
     low, gates, cum, t, wa, wb, u, r, kk, dcum, dkm, maps, adds, sent, got,
     low_sum, beta_cot, rows, packed,
     core_got, core_sum, chip_got, chip_sum, piece_got, total, spread,
@@ -213,11 +215,14 @@
     deep = down_all.shape[1]
     first_rep = deep + per_shard * size
 
+    own = [(down_in, down_all.at[me]), (beta_in, beta_all.at[me])]
+    own += [
+        (up_in.at[:, pl.ds(i * size, size)], up_all.at[me, i]) for i in range(per_shard)
+    ]
+    rest_in = [(hidden_in, hidden), (bias_in, bias), (rate_in, rate), (k_in, k)]
+    rest_in += [(q_in, q), (go_in, go), (s_in, s), (v_in, v)]
     loads = [
-        pltpu.make_async_copy(src, dst, load_sem.at[i])
-        for i, (src, dst) in enumerate(
-            ((hidden_in, hidden), (k_in, k), (q_in, q), (go_in, go), (s_in, s), (v_in, v))
-        )
+        pltpu.make_async_copy(src, dst, load_sem.at[i]) for i, (src, dst) in enumerate(own + rest_in)
     ]
     for c in loads:
         c.start()
@@ -232,10 +237,6 @@
         return 0
 
     lax.fori_loop(1, count_ctx, greet, 0)
-    for i in range(per_shard):
-        up_all[me, i] = up_in[:, i * size : (i + 1) * size]
-    down_all[me] = down_in[...]
-    beta_all[me] = beta_in[...]
     low_sum[...] = jnp.zeros_like(low_sum)
     beta_cot[...] = jnp.zeros_like(beta_cot)
 
@@ -243,35 +244,68 @@
     def _():
         got[...] = jnp.zeros_like(got)
 
+    for c in loads[: len(own)]:
+        c.wait()
     pl.semaphore_wait(barrier, chips + count_ctx - 1)
 
-    def copies(shard, target, slot):
-        return [
-            pltpu.make_async_remote_copy(
-                src_ref=ref.at[shard], dst_ref=ref.at[shard],
-                send_sem=gather_send.at[slot, i], recv_sem=gather_recv.at[slot, i],
-                device_id={"fsdp": target}, device_id_type=MESH,
-            )
-            for i, ref in enumerate((down_all, beta_all, up_all))
-        ]
-
-    for d, peer in enumerate(peers):
-        for c in copies(me, peer, 1 + d):
-            c.start()
-    for c in copies(me, sibling, 0):
-        c.start()
-    for d, source in enumerate(sources):
-        for c, onward in zip(copies(source, peers[d], 1 + d), copies(source, sibling, chips + d)):
-            c.wait_recv()
-            onward.start()
-    for c in copies(sibling, sibling, 0):
-        c.wait_recv()
-    for d, source in enumerate(sources):
-        theirs = (source // 2) * 2 + (1 - core)
-        for c in copies(theirs, sibling, chips + d):
-            c.wait_recv()
-    for c in loads:
+    def weights(shard, target, slot, i):
+        ref = (down_all, beta_all, up_all)[i]
+        return pltpu.make_async_remote_copy(
+            src_ref=ref.at[shard], dst_ref=ref.at[shard],
+            send_sem=gather_send.at[slot, i], recv_sem=gather_recv.at[slot, i],
+            device_id={"fsdp": target}, device_id_type=MESH,
+        )
+
+    def send_own(pieces):
+        for i in pieces:
+            for d, peer in enumerate(peers):
+                weights(me, peer, 1 + d, i).start()
+        for i in pieces:
+            weights(me, sibling, 0, i).start()
+
+    def pass_on(pieces):
+        for i in pieces:
+            for d, source in enumerate(sources):
+                weights(source, peers[d], 1 + d, i).wait_recv()
+                weights(source, sibling, chips + d, i).start()
+        for i in pieces:
+            weights(sibling, sibling, 0, i).wait_recv()
+
+    def take_passed(pieces, d):
+        theirs = (sources[d] // 2) * 2 + (1 - core)
+        for i in pieces:
+            weights(theirs, sibling, chips + d, i).wait_recv()
+
+    send_own((0, 1, 2))
+    pass_on((0, 1))
+    for d in range(chips - 1):
+        take_passed((0, 1), d)
+    by_shard = groups == shards
+    if not by_shard:
+        pass_on((2,))
+        for d in range(chips - 1):
+            take_passed((2,), d)
+    for c in loads[len(own) :]:
         c.wait()
+
+    def order(i):
+        if not by_shard:
+            return i
+        return lax.rem(chip + i // 2, chips) * 2 + lax.rem(core + i, 2)
+
+    def up_ready(i):
+        if not by_shard:
+            return
+
+        @pl.when(i == 1)
+        def _():
+            pass_on((2,))
+
+        for d in range(chips - 1):
+
+            @pl.when(i == 2 * (chips - 1 - d) + 1)
+            def _():
+                take_passed((2,), d)
 
     for shard in range(shards):
         turned = beta_all[shard].astype(F32).T
@@ -297,7 +331,9 @@
 
         @pl.when(mine > 0)
         def _():
-            sent[head] = (adds[head] + mm(maps[head], got[head], NN, 3)).astype(BF16)
+            value = got[head]
+            both = jnp.concatenate([value, value], axis=0)
+            sent[head] = (adds[head] + dot(maps[head], both)).astype(BF16)
             chain_copy(head).start()
 
         return 0
@@ -307,7 +343,8 @@
 
         @pl.when((part >= 0) & (part < groups))
         def _():
-            lax.fori_loop(part * group, part * group + group, chain_turn, 0)
+            at = order(part) * group
+            lax.fori_loop(at, at + group, chain_turn, 0)
 
     def take(g, i):
         head = g * group + i
@@ -317,7 +354,9 @@
     def gate_in(head, at):
         return dot(low[...], up_all[head // per_shard, head % per_shard]) + bias[:, at]
 
-    def first(g, _):
+    def first(turn, _):
+        up_ready(turn)
+        g = order(turn)
         heads = []
         for i in range(group):
             head, at, h = take(g, i)
@@ -326,11 +365,12 @@
         for i, h in enumerate(first_heads(heads)):
             n = g * group + i
             cum[n], kk[n], t[n], wa[n], wb[n] = h["cum"], h["kk"], h["t"], h["wa"].astype(BF16), h["wb"]
-            maps[n], adds[n] = h["map"], h["add"]
-        chain(g)
-        return 0
-
-    def rest(g, _):
+            maps[n], adds[n] = jnp.concatenate(halves(h["map"]), axis=1), h["add"]
+        chain(turn)
+        return 0
+
+    def rest(turn, _):
+        g = order(turn)
         heads = []
         for i in range(group):
             head, at, h = take(g, i)
@@ -341,12 +381,13 @@
             n, at, _ = take(g, i)
             dq[:, at] = h["dq"].astype(BF16)
             u[n], r[n], dcum[n], dkm[n] = h["u"].astype(BF16), h["r"], h["dcum"], h["dkm"]
-        chain(groups + g)
+        chain(groups + turn)
         return 0
 
     lanes = lax.broadcasted_iota(jnp.int32, beta_cot.shape, 1)
 
-    def back(g, _):
+    def back(turn, _):
+        g = order(turn)
         heads = []
         for i in range(group):
             n, at, h = take(g, i)
@@ -364,7 +405,7 @@
             beta_cot[...] += jnp.where(lanes == head, h["dbeta"], 0.0)
             rows[pl.ds(head, 1), :] = h["bias_row"]
             rows[pl.ds(count + head, 1), :] = h["rate_row"]
-        chain(2 * groups + g)
+        chain(2 * groups + turn)
         return 0
 
     stores = [
@@ -484,8 +525,8 @@
     for d, peer in enumerate(peers):
         chip_copy(d, peer).wait_send()
     for slot in range(2 * chips - 1):
-        for c in copies(me, sibling, slot):
-            c.wait_send()
+        for i in range(3):
+            weights(me, sibling, slot, i).wait_send()
 
     @pl.when(mine > 0)
     def _():
@@ -499,8 +540,25 @@
         c.wait()
 
 
-def vmem(count):
-    return [pl.BlockSpec(memory_space=pltpu.VMEM)] * count
+def place_kernel(
+    deep, per_shard, vectors_at,
+    dq, dk, dv, dhidden, summed, dq_out, dk_out, dv_out, dhidden_out, down, up, bias, rate, sem,
+):
+    count, size = bias.shape
+    pairs = [(dq, dq_out), (dk, dk_out), (dv, dv_out), (dhidden, dhidden_out)]
+    pairs += [(summed.at[pl.ds(0, deep)], down)]
+    rank = up.shape[0]
+    pairs += [
+        (summed.at[pl.ds(deep + i * rank, rank)], up.at[:, pl.ds(i * size, size)])
+        for i in range(per_shard)
+    ]
+    pairs += [(summed.at[pl.ds(vectors_at, count)], bias)]
+    pairs += [(summed.at[pl.ds(vectors_at + count, count)], rate)]
+    copies = [pltpu.make_async_copy(src, dst, sem.at[i]) for i, (src, dst) in enumerate(pairs)]
+    for c in copies:
+        c.start()
+    for c in copies:
+        c.wait()
 
 
 def remote(collective):
@@ -551,23 +609,24 @@
             jax.ShapeDtypeStruct((tokens, width), BF16),
             jax.ShapeDtypeStruct((rows, size), F32),
         ),
-        in_specs=[anywhere] * 6 + vmem(5),
+        in_specs=[anywhere] * 11,
         out_specs=(anywhere,) * 4 + (pl.BlockSpec(memory_space=pltpu.VMEM),),
         scratch_shapes=[
+            pltpu.VMEM((1, channels), F32), pltpu.VMEM((1, channels), F32),
             sized, sided, sided, sided, sided, states_f32, sided, sided, sided, sized,
             pltpu.VMEM((shards, deep, rank), BF16),
             pltpu.VMEM((shards, per_shard, rank, size), BF16),
             pltpu.VMEM((shards, count, wide), BF16), pltpu.VMEM((width, count), BF16),
             pltpu.VMEM((tokens, rank), BF16), pltpu.VMEM((tokens, count), F32),
             heads_f32, mixed, heads_bf16, heads_f32, heads_bf16, heads_f32, mixed, heads_f32, heads_f32,
-            states_f32, states_f32, states_bf16, states_bf16,
+            pltpu.VMEM((count, size, 2 * size), BF16), states_f32, states_bf16, states_bf16,
             pltpu.VMEM((tokens, rank), F32), pltpu.VMEM((tokens, count), F32),
             pltpu.VMEM((2 * count, size), F32), pltpu.VMEM((shards, rows, size), BF16),
             pltpu.VMEM((chips, rows, size), BF16), pltpu.VMEM((chips, rows, size), BF16),
             pltpu.VMEM((far, rows, size), BF16), pltpu.VMEM((rows, size), BF16),
             pltpu.VMEM((blocks_ctx - 1, piece, size), BF16), pltpu.VMEM((piece, size), BF16),
             pltpu.VMEM((blocks_ctx - 1, piece, size), BF16),
-            dma((6,)), dma((4,)), dma((2 * chips - 1, 3)), dma((2 * chips - 1, 3)),
+            dma((10 + per_shard,)), dma((4,)), dma((2 * chips - 1, 3)), dma((2 * chips - 1, 3)),
             dma((count,)), dma((count,)),
             dma((chips,)), dma((chips,)), dma((far,)), dma((far,)),
             dma((blocks_ctx - 1,)), dma((blocks_ctx - 1,)),
@@ -579,14 +638,30 @@
 
     up_at = deep + per_shard * size
     beta_at = up_at + (width // size) * count
-    up_grad = summed[deep:up_at].reshape(per_shard, rank, size).swapaxes(0, 1).reshape(rank, -1)
+    flat = jax.ShapeDtypeStruct((count, size), F32)
+    dq, dk, dv, dhidden, down_grad, up_grad, bias_grad, rate_grad = pl.pallas_call(
+        functools.partial(place_kernel, deep, per_shard, beta_at),
+        out_shape=(
+            jax.ShapeDtypeStruct((tokens, channels), BF16),
+            jax.ShapeDtypeStruct((tokens, channels), BF16),
+            jax.ShapeDtypeStruct((tokens, channels), BF16),
+            jax.ShapeDtypeStruct((tokens, width), BF16),
+            jax.ShapeDtypeStruct((deep, rank), F32),
+            jax.ShapeDtypeStruct((rank, per_shard * size), F32),
+            flat, flat,
+        ),
+        in_specs=[anywhere] * 5,
+        out_specs=(anywhere,) * 8,
+        scratch_shapes=[dma((7 + per_shard,))],
+        compiler_params=pltpu.CompilerParams(vmem_limit_bytes=VMEM_LIMIT),
+        name="place_results",
+    )(dq, dk, dv, dhidden, summed)
     beta_rows = summed[up_at:beta_at].reshape(width // size, count, size)
     beta_full = beta_rows.swapaxes(1, 2).reshape(width, count)
     beta_grad = lax.dynamic_slice_in_dim(beta_full, lax.axis_index("fsdp") * deep, deep, 0)
-    vectors = summed[beta_at : beta_at + 2 * count].reshape(2, count * size)
     return (
         dq[None], dk[None], dv[None], dhidden[None],
-        summed[:deep], up_grad, beta_grad, vectors[0], vectors[1],
+        down_grad, up_grad, beta_grad, bias_grad.reshape(-1), rate_grad.reshape(-1),
     )
 
 

time: 100 us -> 171 us (1.71)
  Pallas kernels: 84.4 us -> 167 us
  local copies, waits for them, and re-layouts: 14.5 us -> 3.05 us
    pallas_call x0 -> x1, Pallas kernels: none -> 84.1 us  [on_device(): pl.pallas_call(functools.partial(place_kernel, deep, per_shard, beta_at),...]
    unnamed x25 -> x1, local copies, waits for them, and re-layouts: 11.7 us -> 0.03 us
where the time goes in v3:
time: 171 us
  Pallas kernels  167 us (98%)
  local copies, waits for them, and re-layouts  3.05 us (2%)
    pallas_call x1, Pallas kernels, on_device(): pl.pallas_call(functools.partial(place_kernel, deep, per_shard, beta_at),...  84.1 us
    pallas_call x1, Pallas kernels, on_device(): pl.pallas_call(functools.partial(fused_kernel, shards, blocks_ctx, group)...  83.2 us

profile of v3, /device:TPU:0, one launch (start us, length us, event | category | flops | bytes accessed | tf_op | source)
XLA Modules:
  0.0 171.0 jit_solution(16758469881170474648)
XLA Ops:
  0.6 1.3 pad.4.beta_in
  2.0 83.2 %delta_backward.1 = (bf16[128,2048]{1,0:T(8,128)(2,1)}, bf16[128,2048]{1,0:T(8,128)(2,1)}, bf16[128,2048]{1,0:T(8,128)(2,1)}, bf16[128,2304]{1,0:T(8,128)(2,1)}, f32[1408,128]{1,0:T(8,128)}) custom-call(bf16[128,2304]{1,0:T(8,128)(2,1)} %bitcast.25, bf16[128,2048]{1,0:T(8,128)(2,1)} %bitcast.27, bf16[128,2048]{1,0:T(8,128)(2,1)} %bitcast.28, ...), custom_call_target="tpu_custom_call" | custom-call | tf_op jit(solution)/shard_map/delta_backward/pallas_call | solution.py:603
  85.2 84.1 %place_results.1 = (bf16[128,2048]{1,0:T(8,128)(2,1)}, bf16[128,2048]{1,0:T(8,128)(2,1)}, bf16[128,2048]{1,0:T(8,128)(2,1)}, bf16[128,2304]{1,0:T(8,128)(2,1)}, ...) custom-call(bf16[128,2048]{1,0:T(8,128)(2,1)} %get-tuple-element.22.dq, ...), custom_call_target="tpu_custom_call" | custom-call | tf_op jit(solution)/shard_map/place_results/pallas_call | solution.py:642
  169.3 0.9 slice.3
  170.2 0.1 copy.21
  170.3 0.7 constant_dynamic-slice_fusion
  (1 shorter events, 0.0 us)

commit v4 on v3

--- a/solution.py
+++ b/solution.py
@@ -309,7 +309,7 @@
 
     for shard in range(shards):
         turned = beta_all[shard].astype(F32).T
-        beta_full[shard * deep : (shard + 1) * deep, :] = turned[:deep].astype(BF16)
+        beta_full[shard * deep : (shard + 1) * deep, :] = turned.astype(BF16)
     low[...] = dot(hidden[...], down_all[...].reshape(shards * deep, -1)).astype(BF16)
     gates[...] = sigmoid(dot(hidden[...], beta_full[...]))
 
@@ -542,20 +542,30 @@
 
 def place_kernel(
     deep, per_shard, vectors_at,
-    dq, dk, dv, dhidden, summed, dq_out, dk_out, dv_out, dhidden_out, down, up, bias, rate, sem,
+    dq, dk, dv, dhidden, summed, dq_out, dk_out, dv_out, dhidden_out, down, up, bias, rate,
+    dq_held, dk_held, dv_held, dhidden_held, held, load_sem, sem,
 ):
     count, size = bias.shape
-    pairs = [(dq, dq_out), (dk, dk_out), (dv, dv_out), (dhidden, dhidden_out)]
-    pairs += [(summed.at[pl.ds(0, deep)], down)]
+    loads = [(summed, held), (dq, dq_held), (dk, dk_held), (dv, dv_held), (dhidden, dhidden_held)]
+    loads = [pltpu.make_async_copy(src, dst, load_sem.at[i]) for i, (src, dst) in enumerate(loads)]
+    for c in loads:
+        c.start()
+    pairs = [(held.at[pl.ds(0, deep)], down)]
     rank = up.shape[0]
     pairs += [
-        (summed.at[pl.ds(deep + i * rank, rank)], up.at[:, pl.ds(i * size, size)])
+        (held.at[pl.ds(deep + i * rank, rank)], up.at[:, pl.ds(i * size, size)])
         for i in range(per_shard)
     ]
-    pairs += [(summed.at[pl.ds(vectors_at, count)], bias)]
-    pairs += [(summed.at[pl.ds(vectors_at + count, count)], rate)]
+    pairs += [(held.at[pl.ds(vectors_at, count)], bias)]
+    pairs += [(held.at[pl.ds(vectors_at + count, count)], rate)]
+    first = len(pairs)
+    pairs += [(dq_held, dq_out), (dk_held, dk_out), (dv_held, dv_out), (dhidden_held, dhidden_out)]
     copies = [pltpu.make_async_copy(src, dst, sem.at[i]) for i, (src, dst) in enumerate(pairs)]
-    for c in copies:
+    loads[0].wait()
+    for c in copies[:first]:
+        c.start()
+    for load, c in zip(loads[1:], copies[first:]):
+        load.wait()
         c.start()
     for c in copies:
         c.wait()
@@ -589,8 +599,7 @@
     rows = -(-rows // unit_size) * unit_size
     piece = rows // blocks_ctx
     far = max(chips - 1, 1)
-    wide = -(-deep // size) * size
-    beta_t = jnp.pad(beta_weight.T, ((0, 0), (0, wide - deep)))
+    beta_t = beta_weight.T
     channels = count * size
     anywhere = pl.BlockSpec(memory_space=pl.ANY)
     heads_f32 = pltpu.VMEM((count, tokens, size), F32)
@@ -616,7 +625,7 @@
             sized, sided, sided, sided, sided, states_f32, sided, sided, sided, sized,
             pltpu.VMEM((shards, deep, rank), BF16),
             pltpu.VMEM((shards, per_shard, rank, size), BF16),
-            pltpu.VMEM((shards, count, wide), BF16), pltpu.VMEM((width, count), BF16),
+            pltpu.VMEM((shards, count, deep), BF16), pltpu.VMEM((width, count), BF16),
             pltpu.VMEM((tokens, rank), BF16), pltpu.VMEM((tokens, count), F32),
             heads_f32, mixed, heads_bf16, heads_f32, heads_bf16, heads_f32, mixed, heads_f32, heads_f32,
             pltpu.VMEM((count, size, 2 * size), BF16), states_f32, states_bf16, states_bf16,
@@ -652,7 +661,7 @@
         ),
         in_specs=[anywhere] * 5,
         out_specs=(anywhere,) * 8,
-        scratch_shapes=[dma((7 + per_shard,))],
+        scratch_shapes=[sided, sided, sided, sized, pltpu.VMEM((rows, size), F32), dma((5,)), dma((7 + per_shard,))],
         compiler_params=pltpu.CompilerParams(vmem_limit_bytes=VMEM_LIMIT),
         name="place_results",
     )(dq, dk, dv, dhidden, summed)

time: 171 us -> 88.6 us (0.52)
  Pallas kernels: 167 us -> 86.1 us
    pallas_call x1, Pallas kernels: 84.1 us -> 2.77 us  [on_device(): pl.pallas_call(functools.partial(place_kernel, deep, per_shard, beta_at),...]
where the time goes in v4:
time: 88.6 us; the launch traced here: 88.5 us
  Pallas kernels  86.1 us (97%)
  local copies, waits for them, and re-layouts  1.71 us (2%)
    pallas_call x1, Pallas kernels, on_device(): pl.pallas_call(functools.partial(fused_kernel, shards, blocks_ctx, group)...  83.3 us
    pallas_call x1, Pallas kernels, on_device(): pl.pallas_call(functools.partial(place_kernel, deep, per_shard, beta_at),...  2.77 us

profile of v4, /device:TPU:0, one launch (start us, length us, event | category | flops | bytes accessed | tf_op | source)
XLA Modules:
  0.0 88.5 jit_solution(13757988773896867669)
XLA Ops:
  0.6 83.3 %delta_backward.1 = (bf16[128,2048]{1,0:T(8,128)(2,1)}, bf16[128,2048]{1,0:T(8,128)(2,1)}, bf16[128,2048]{1,0:T(8,128)(2,1)}, bf16[128,2304]{1,0:T(8,128)(2,1)}, f32[1408,128]{1,0:T(8,128)}) custom-call(bf16[128,2304]{1,0:T(8,128)(2,1)} %bitcast.25, bf16[128,2048]{1,0:T(8,128)(2,1)} %bitcast.27, bf16[128,2048]{1,0:T(8,128)(2,1)} %bitcast.28, ...), custom_call_target="tpu_custom_call" | custom-call | tf_op jit(solution)/shard_map/delta_backward/pallas_call | solution.py:612
  83.9 2.8 %place_results.1 = (bf16[128,2048]{1,0:T(8,128)(2,1)}, bf16[128,2048]{1,0:T(8,128)(2,1)}, bf16[128,2048]{1,0:T(8,128)(2,1)}, bf16[128,2304]{1,0:T(8,128)(2,1)}, ...) custom-call(bf16[128,2048]{1,0:T(8,128)(2,1)} %get-tuple-element.22.dq, ...), custom_call_target="tpu_custom_call" | custom-call | tf_op jit(solution)/shard_map/place_results/pallas_call | solution.py:651
  86.7 0.9 %slice.3 = f32[288,128]{1,0:T(8,128)S(1)} slice(f32[1408,128]{1,0:T(8,128)} %get-tuple-element.26.summed), slice={[1088:1376], [0:128]} | slice | bytes 294912 | tf_op jit(solution)/shard_map/slice | solution.py:668
  87.7 0.1 copy.21
  87.7 0.7 constant_dynamic-slice_fusion
  (1 shorter events, 0.0 us)
